TPU v7x, 32 devices: a whole 2x2x4 slice. The times are simulated.
32 devices in a mesh: seq: 2 (over y), exp: 16 (over z, x, core).
Axes of the slice: x: 2, y: 2, z: 4, core: 2. Of those that a mesh axis runs over, the one named last changes fastest.
Arguments:
- stream_input: bfloat16 [16, 256, 2048], P('exp', 'seq'), may hold values from -40 to 40
- grad_output: bfloat16 [16, 256, 2048], P('exp', 'seq'), may hold values from -6 to 6
- norm_gain: float32 [2048], replicated, may hold values from 0.1 to 1.9
- routes: int32 [16, 256, 6], P('exp', 'seq'), may hold values from 0 to 15, all different within a row; in each aligned block of 128 rows (0 to 127, 128 to 255, ..., all dimensions but the last counted through in order) at most 57 rows name the same one
- gates: float32 [16, 256, 6], P('exp', 'seq'), may hold values from 0.1 to 0.6
- w_gate: bfloat16 [16, 2048, 704], P('exp'), may hold values from -0.125 to 0.125
- w_up: bfloat16 [16, 2048, 704], P('exp'), may hold values from -0.125 to 0.125
- w_down: bfloat16 [16, 704, 2048], P('exp'), may hold values from -0.21875 to 0.21875
- ssd_input: bfloat16 [16, 256, 2048], P('exp', 'seq'), may hold values from -0.75 to 0.75
- in_keys: bfloat16 [16, 256, 128], P('exp', 'seq'), may hold values from -6 to 6
- out_queries: bfloat16 [16, 256, 128], P('exp', 'seq'), may hold values from -0.03125 to 0.03125
- log_decay: float32 [16, 256, 32], P('exp', 'seq'), may hold values from -1 to 0
Outputs:
- grad_stream: bfloat16 [16, 256, 2048], P('exp', 'seq')
- grad_x: bfloat16 [16, 256, 2048], P('exp', 'seq')
- grad_b: float32 [16, 256, 128], P('exp', 'seq')
Inputs may be any that keep to these rules, and one draw needn't show every extreme that they name: `routes`: each token names 6 different experts; among the 128 tokens of one device no expert is named more than 57 times, a bound that some block reaches.
All inputs are finite; a program needn't handle non-finite values.
Results may differ from a plain program's by a relative error of at most 0.0075.
Values may be sent and summed in bfloat16 or wider, within the bound.
A program may use at most 128 MiB of HBM per device.

v0:
```python
import jax
import jax.numpy as jnp
from jax import lax
from jax.sharding import PartitionSpec as P

TOPK = 6


EXACT_PRODUCT = lax.Precision.HIGHEST
EPSILON = 1e-05


def carried_in(shard, axis, join, neutral):
    count = lax.axis_size(axis)
    place = lax.axis_index(axis)
    ahead = count - 1 - place
    gathered = jax.tree.map(
        lambda a, kind: lax.all_gather(a.astype(kind), axis), shard, (jnp.bfloat16, jnp.bfloat16)
    )
    state = jax.tree.map(lambda a, e: jnp.zeros_like(a) + jnp.asarray(e, a.dtype), shard, neutral)

    def one(lap, state):
        source = count - 1 - lap
        return join(
            state,
            jax.tree.map(
                lambda a, own: lax.dynamic_index_in_dim(a, source, 0, False).astype(own.dtype),
                gathered,
                shard,
            ),
        )

    return lax.fori_loop(0, ahead, one, state)


def assign_slots(flat_routes, expert_count):
    onehot_table = (
        flat_routes[:, None] == jnp.arange(expert_count, dtype=jnp.int32)[None, :]
    ).astype(jnp.int32)
    earlier_hits = jnp.cumsum(onehot_table, axis=0) - onehot_table
    return jnp.sum(earlier_hits * onehot_table, axis=1)


def transposed_product(left_rows, weight_matrix):
    return lax.dot_general(
        left_rows, weight_matrix, (((1,), (1,)), ((), ())), preferred_element_type=jnp.float32
    )


def expert_back(normed_rows, grad_rows, gate_weight, up_weight, down_weight):
    gate_pre = jnp.dot(normed_rows, gate_weight, preferred_element_type=jnp.float32)
    up_pre = jnp.dot(normed_rows, up_weight, preferred_element_type=jnp.float32)
    back_rows = transposed_product(grad_rows, down_weight)
    sigmoid_gate = jax.nn.sigmoid(gate_pre)
    grad_gate = (
        back_rows * up_pre * sigmoid_gate * (1.0 + gate_pre * (1.0 - sigmoid_gate))
    ).astype(jnp.bfloat16)
    grad_up = (back_rows * gate_pre * sigmoid_gate).astype(jnp.bfloat16)
    summed = transposed_product(grad_gate, gate_weight) + transposed_product(grad_up, up_weight)
    return summed.astype(jnp.bfloat16)


def block_terms(out_grad, inputs, key_rows, query_rows, decay_rows):
    row_count = out_grad.shape[0]
    head_count = decay_rows.shape[1]
    cum_decay = jnp.cumsum(decay_rows, axis=0)
    by_head = cum_decay.T
    later_mask = (jnp.arange(row_count)[None, :] >= jnp.arange(row_count)[:, None])[None]
    differences = by_head[:, None, :] - by_head[:, :, None]
    decay_matrix = jnp.where(later_mask, jnp.exp(jnp.where(later_mask, differences, -1e30)), 0.0)
    scores = jnp.dot(key_rows, query_rows.T, precision=EXACT_PRODUCT)
    grad_heads = out_grad.reshape(row_count, head_count, -1)
    input_heads = inputs.reshape(row_count, head_count, -1)
    head_size = grad_heads.shape[2]
    intra_x = jnp.einsum(
        "hts,shp->thp", decay_matrix * scores[None], grad_heads, precision=EXACT_PRODUCT
    ).reshape(row_count, -1)
    pair_mix = jnp.einsum("thp,shp->hts", input_heads, grad_heads, precision=EXACT_PRODUCT)
    intra_b = jnp.dot(jnp.sum(decay_matrix * pair_mix, axis=0), query_rows, precision=EXACT_PRODUCT)
    weighted = out_grad * jnp.repeat(jnp.exp(cum_decay), head_size, axis=1)
    local_state = jnp.dot(query_rows.T, weighted, precision=EXACT_PRODUCT)
    decay_total = cum_decay[-1]
    edge_decay = jnp.repeat(jnp.exp(cum_decay[-1][None, :] - cum_decay), head_size, axis=1)
    return (intra_x, intra_b, local_state, decay_total, edge_decay)


def remote_terms(incoming, key_rows, inputs, edge_decay):
    remote_x = edge_decay * jnp.dot(key_rows, incoming, precision=EXACT_PRODUCT)
    remote_b = jnp.dot(inputs * edge_decay, incoming.T, precision=EXACT_PRODUCT)
    return (remote_x, remote_b)


def combine_blocks(earlier, later):
    earlier_total, earlier_state = earlier
    later_total, later_state = later
    factor = jnp.repeat(jnp.exp(later_total), later_state.shape[1] // later_total.shape[0])[None, :]
    return (earlier_total + later_total, later_state + factor * earlier_state)


def local(
    stream_input,
    grad_output,
    norm_gain,
    routes,
    gates,
    w_gate,
    w_up,
    w_down,
    ssd_input,
    in_keys,
    out_queries,
    log_decay,
):
    token_count = stream_input.shape[1]
    width = stream_input.shape[2]
    state_size = in_keys.shape[2]
    head_count = log_decay.shape[2]
    expert_count = lax.axis_size("exp")
    capacity = token_count * 7 // expert_count + 1
    stream_rows = stream_input.reshape(token_count, width).astype(jnp.float32)
    root_mean = jnp.sqrt(jnp.mean(stream_rows * stream_rows, axis=1, keepdims=True) + EPSILON)
    unit_rows = stream_rows / root_mean
    normed = (unit_rows * norm_gain[None, :]).astype(jnp.bfloat16)
    grad_rows = grad_output.reshape(token_count, width)
    flat_routes = routes.reshape(token_count * TOPK)
    slots = assign_slots(flat_routes, expert_count)
    destination = flat_routes * capacity + slots
    send_normed = (
        jnp.zeros((expert_count * capacity, width), jnp.bfloat16)
        .at[destination]
        .set(jnp.repeat(normed, TOPK, axis=0))
        .reshape(expert_count, capacity, width)
    )
    send_grads = (
        jnp.zeros((expert_count * capacity, width), jnp.bfloat16)
        .at[destination]
        .set(jnp.repeat(grad_rows, TOPK, axis=0))
        .reshape(expert_count, capacity, width)
    )
    gate_weight = w_gate[0]
    up_weight = w_up[0]
    down_weight = w_down[0]
    normed_part = lax.all_to_all(send_normed, "exp", split_axis=0, concat_axis=0, tiled=True)
    grad_part = lax.all_to_all(send_grads, "exp", split_axis=0, concat_axis=0, tiled=True)
    sources = normed_part.shape[0]
    slot_count = normed_part.shape[1]
    result_rows = expert_back(
        normed_part.reshape(sources * slot_count, width),
        grad_part.reshape(sources * slot_count, width),
        gate_weight,
        up_weight,
        down_weight,
    ).reshape(sources, slot_count, width)
    expert_result = result_rows
    expert_result = lax.all_to_all(expert_result, "exp", split_axis=0, concat_axis=0, tiled=True)
    picked = expert_result.reshape(expert_count * capacity, width)[destination].reshape(
        token_count, TOPK, width
    )
    normed_grad = jnp.sum(gates.reshape(token_count, TOPK, 1) * picked.astype(jnp.float32), axis=1)
    scaled = normed_grad * norm_gain[None, :]
    stream_grad = (
        grad_rows.astype(jnp.float32)
        + (scaled - unit_rows * jnp.mean(unit_rows * scaled, axis=1, keepdims=True)) / root_mean
    ).astype(jnp.bfloat16)
    inputs = ssd_input.reshape(token_count, width).astype(jnp.float32)
    key_rows = in_keys.reshape(token_count, state_size).astype(jnp.float32)
    query_rows = out_queries.reshape(token_count, state_size).astype(jnp.float32)
    decay_rows = log_decay.reshape(token_count, head_count)
    intra_x, intra_b, local_state, decay_total, edge_decay = block_terms(
        stream_grad.astype(jnp.float32), inputs, key_rows, query_rows, decay_rows
    )
    summed_total, incoming = carried_in(
        (decay_total, local_state),
        "seq",
        combine_blocks,
        (jnp.zeros_like(decay_total), jnp.zeros_like(local_state)),
    )
    remote_x, remote_b = remote_terms(incoming, key_rows, inputs, edge_decay)
    grad_x = (intra_x + remote_x).astype(jnp.bfloat16).reshape(1, token_count, width)
    grad_b = (intra_b + remote_b).reshape(1, token_count, state_size)
    return (stream_grad.reshape(1, token_count, width), grad_x, grad_b)


def solution(mesh):
    placed = (
        P("exp", "seq", None),
        P("exp", "seq", None),
        P(),
        P("exp", "seq", None),
        P("exp", "seq", None),
        P("exp", None, None),
        P("exp", None, None),
        P("exp", None, None),
        P("exp", "seq", None),
        P("exp", "seq", None),
        P("exp", "seq", None),
        P("exp", "seq", None),
    )
    return jax.shard_map(
        local,
        mesh=mesh,
        in_specs=placed,
        out_specs=(P("exp", "seq", None), P("exp", "seq", None), P("exp", "seq", None)),
        check_vma=False,
    )
```

profile of v0, /device:TPU:10, one launch (start us, length us, event | category | flops | bytes accessed | tf_op | source)
XLA Modules:
  0.0 442.6 jit_solution(4237933370424319876)
XLA Ops:
  7.2 0.9 copy.66
  8.4 0.7 broadcast_multiply_fusion
  9.1 1.7 reduce-window.6
  11.4 1.2 fusion.28
  12.6 1.3 multiply_convert_fusion.3
  13.9 2.6 broadcast_in_dim.58
  16.5 6.3 %reshape.372 = bf16[768,2048]{1,0:T(8,128)(2,1)} reshape(bf16[128,6,2048]{2,1,0:T(8,128)(2,1)} %broadcast_in_dim.58) | data formatting | bytes 6291456 | tf_op jit(solution)/shard_map/reshape | solution.py:131
  22.9 10.2 %scatter_custom_fusion.1 = bf16[912,2048]{1,0:T(8,128)(2,1)} fusion(s32[768]{0:T(1024)S(1)} %fusion.49, bf16[768,2048]{1,0:T(8,128)(2,1)} %reshape.372, bf16[]{:T(256)} %constant.52.clone.1), kind=kCustom, calls=%fused_computation.31 | custom fusion | bytes 3736064 | tf_op jit(solution)/shard_map/scatter | solution.py:131
  33.1 4.1 reshape.334
  37.1 6.7 %all-to-all-start.1 = ((bf16[16,57,2048]{2,1,0:T(8,128)(2,1)}), bf16[16,57,2048]{2,1,0:T(8,128)(2,1)}, u32[]{:S(2)}, u32[]{:S(2)}) async-start(bf16[16,57,2048]{2,1,0:T(8,128)(2,1)} %reshape.334), calls=%async_computation.1 | async-start | bytes 8388608 | tf_op jit(solution)/shard_map/all_to_all | solution.py:143
  43.9 2.6 broadcast_in_dim.57
  46.5 6.3 %reshape.364 = bf16[768,2048]{1,0:T(8,128)(2,1)} reshape(bf16[128,6,2048]{2,1,0:T(8,128)(2,1)} %broadcast_in_dim.57) | data formatting | bytes 6291456 | tf_op jit(solution)/shard_map/reshape | solution.py:137
  52.8 10.2 %scatter_custom_fusion = bf16[912,2048]{1,0:T(8,128)(2,1)} fusion(s32[768]{0:T(1024)S(1)} %fusion.49, bf16[768,2048]{1,0:T(8,128)(2,1)} %reshape.364, bf16[]{:T(256)} %constant.52.clone.1), kind=kCustom, calls=%fused_computation.33 | custom fusion | bytes 3736064 | tf_op jit(solution)/shard_map/scatter | solution.py:137
  63.0 4.1 reshape.331
  67.1 69.0 %all-to-all-done.1 = bf16[16,57,2048]{2,1,0:T(8,128)(2,1)} async-done(((bf16[16,57,2048]{2,1,0:T(8,128)(2,1)}), bf16[16,57,2048]{2,1,0:T(8,128)(2,1)}, u32[]{:S(2)}, u32[]{:S(2)}) %all-to-all-start.1) | async-done | bytes 3735584 | tf_op jit(solution)/shard_map/all_to_all | solution.py:143
  136.0 5.4 %all-to-all-start = ((bf16[16,57,2048]{2,1,0:T(8,128)(2,1)}), bf16[16,57,2048]{2,1,0:T(8,128)(2,1)}, u32[]{:S(2)}, u32[]{:S(2)}) async-start(bf16[16,57,2048]{2,1,0:T(8,128)(2,1)} %reshape.331), calls=%async_computation | async-start | bytes 8388608 | tf_op jit(solution)/shard_map/all_to_all | solution.py:144
  141.4 4.1 reshape.335
  145.5 7.6 %fusion.2 = f32[912,704]{1,0:T(8,128)} fusion(bf16[912,2048]{1,0:T(8,128)(2,1)} %reshape.335, bf16[1,2048,704]{1,2,0:T(8,128)(2,1)} %param.19), kind=kOutput, calls=%fused_computation.9 | convolution fusion | flops 2629828608 | bytes 9187328 | tf_op jit(solution)/shard_map/dot_general | solution.py:51
  153.1 80.5 %all-to-all-done = bf16[16,57,2048]{2,1,0:T(8,128)(2,1)} async-done(((bf16[16,57,2048]{2,1,0:T(8,128)(2,1)}), bf16[16,57,2048]{2,1,0:T(8,128)(2,1)}, u32[]{:S(2)}, u32[]{:S(2)}) %all-to-all-start) | async-done | bytes 3735584 | tf_op jit(solution)/shard_map/all_to_all | solution.py:144
  233.6 4.0 reshape.332
  237.6 7.6 %fusion.7 = f32[912,704]{1,0:T(8,128)} fusion(bf16[912,2048]{1,0:T(8,128)(2,1)} %reshape.332, bf16[1,704,2048]{2,1,0:T(8,128)(2,1)} %param.21), kind=kOutput, calls=%fused_computation.14 | convolution fusion | flops 2629828608 | bytes 9187328 | tf_op jit(solution)/shard_map/dot_general | solution.py:45
  245.3 12.8 %fusion = f32[912,2048]{1,0:T(8,128)} fusion(bf16[1,2048,704]{1,2,0:T(8,128)(2,1)} %param.19, f32[912,704]{1,0:T(8,128)} %fusion.2, f32[912,704]{1,0:T(8,128)} %fusion.7, bf16[912,2048]{1,0:T(8,128)(2,1)} %reshape.335, bf16[1,2048,704]{1,2,0:T(8,128)(2,1)S(1)} %copy-done), kind=kOutput, calls=%fused_computation.7 | convolution fusion | flops 5266077696 | bytes 22110208 | tf_op jit(solution)/shard_map/dot_general | solution.py:45
  258.1 8.4 %add_convert_fusion = bf16[912,2048]{1,0:T(8,128)(2,1)} fusion(f32[912,2048]{1,0:T(8,128)} %fusion, bf16[1,2048,704]{1,2,0:T(8,128)(2,1)S(1)} %copy-done, f32[912,704]{1,0:T(8,128)} %fusion.7, f32[912,704]{1,0:T(8,128)} %fusion.2), kind=kOutput, calls=%fused_computation.6 | convolution fusion | flops 2637416448 | bytes 19226624 | tf_op jit(solution)/shard_map/dot_general | solution.py:45
  266.4 4.1 reshape.336
  270.5 5.2 %all-to-all-start.2 = ((bf16[16,57,2048]{2,1,0:T(8,128)(2,1)}), bf16[16,57,2048]{2,1,0:T(8,128)(2,1)}, u32[]{:S(2)}, u32[]{:S(2)}) async-start(bf16[16,57,2048]{2,1,0:T(8,128)(2,1)} %reshape.336), calls=%async_computation.2 | async-start | bytes 8388608 | tf_op jit(solution)/shard_map/all_to_all | solution.py:155
  276.0 4.5 %all-gather.1 = bf16[2,1,32]{2,1,0:T(2,128)(2,1)S(1)} all-gather(bf16[1,1,32]{2,1,0:T(2,128)(2,1)S(1)} %convert_bitcast_fusion), channel_id=1, replica_groups=mesh['seq'=2,'exp'=16] {'seq'}, dimensions={0}, use_global_device_ids=true | all-gather | bytes 192 | tf_op jit(solution)/shard_map/all_gather | solution.py:18
  280.7 1.3 copy.71
  282.7 1.1 bitcast_multiply_fusion.1
  284.0 84.0 %all-to-all-done.2 = bf16[16,57,2048]{2,1,0:T(8,128)(2,1)} async-done(((bf16[16,57,2048]{2,1,0:T(8,128)(2,1)}), bf16[16,57,2048]{2,1,0:T(8,128)(2,1)}, u32[]{:S(2)}, u32[]{:S(2)}) %all-to-all-start.2) | async-done | bytes 3735584 | tf_op jit(solution)/shard_map/all_to_all | solution.py:155
  368.0 4.1 reshape.337
  372.0 9.6 %gather_fusion = bf16[768,2048]{1,0:T(8,128)(2,1)} fusion(bf16[912,2048]{1,0:T(8,128)(2,1)} %reshape.337, s32[1024]{0:T(1024)S(1)} %pad_clamp_fusion), kind=kCustom, calls=%fused_computation | custom fusion | bytes 6294528 | tf_op jit(solution)/shard_map/gather | solution.py:156
  381.7 6.6 %reshape.348 = f32[128,6,2048]{2,1,0:T(8,128)} reshape(bf16[768,2048]{1,0:T(8,128)(2,1)} %gather_fusion) | data formatting | bytes 9437184 | tf_op jit(solution)/shard_map/convert_element_type | solution.py:159
  388.2 6.5 %multiply_reduce_fusion = f32[128,2048]{1,0:T(8,128)S(1)} fusion(f32[128,6,2048]{2,1,0:T(8,128)} %reshape.348, f32[128,6]{1,0:T(8,128)S(1)} %bitcast.143), kind=kLoop, calls=%fused_computation.5 | loop fusion | flops 2883584 | bytes 7343104 | tf_op jit(solution)/shard_map/reduce_sum | solution.py:159
  394.8 0.3 multiply_reduce_fusion.1
  395.1 1.3 copy.70
  396.4 2.8 convert_multiply_fusion
  399.2 1.4 fusion.13
  400.6 2.2 fusion.14
  403.1 2.6 fusion.15
  405.7 1.2 fusion.34
  406.9 15.1 %all-gather.4.cloned.1.call-done = bf16[256,2048]{0,1:T(8,128)(2,1)} async-done(((bf16[128,2048]{0,1:T(8,128)(2,1)}), bf16[256,2048]{0,1:T(8,128)(2,1)}) %all-gather.4.cloned.1.call-update) | async-done | bytes 1048592 | tf_op jit(solution)/shard_map/all_gather | solution.py:18
  422.0 1.5 copy.86
  423.5 1.1 broadcast_in_dim.63
  424.7 2.8 while.14
  424.8 2.4 convert_add_fusion.2
  427.6 2.7 fusion.12
  430.3 1.0 copy.82
  431.3 4.0 fusion.24
  (58 shorter events, 2.8 us)
Async XLA Ops:
  7.2 238.1 %copy-start = (bf16[1,2048,704]{1,2,0:T(8,128)(2,1)S(1)}, bf16[1,2048,704]{1,2,0:T(8,128)(2,1)}, u32[]{:S(2)}) copy-start(bf16[1,2048,704]{1,2,0:T(8,128)(2,1)} %param.20) | copy-start | bytes 8650756
  37.1 6.7 %copy-start.3 = (bf16[1,128,2048]{2,1,0:T(8,128)(2,1)S(1)}, bf16[1,128,2048]{2,1,0:T(8,128)(2,1)}, u32[]{:S(2)}) copy-start(bf16[1,128,2048]{2,1,0:T(8,128)(2,1)} %param.15) | copy-start | bytes 1572868
  37.1 98.9 %all-to-all-start.1 = ((bf16[16,57,2048]{2,1,0:T(8,128)(2,1)}), bf16[16,57,2048]{2,1,0:T(8,128)(2,1)}, u32[]{:S(2)}, u32[]{:S(2)}) async-start(bf16[16,57,2048]{2,1,0:T(8,128)(2,1)} %reshape.334), calls=%async_computation.1 | async-start | bytes 8388608 | tf_op jit(solution)/shard_map/all_to_all | solution.py:143
  136.0 97.6 %all-to-all-start = ((bf16[16,57,2048]{2,1,0:T(8,128)(2,1)}), bf16[16,57,2048]{2,1,0:T(8,128)(2,1)}, u32[]{:S(2)}, u32[]{:S(2)}) async-start(bf16[16,57,2048]{2,1,0:T(8,128)(2,1)} %reshape.331), calls=%async_computation | async-start | bytes 8388608 | tf_op jit(solution)/shard_map/all_to_all | solution.py:144
  270.5 5.3 %copy-start.10 = (f32[1,128,32]{1,2,0:T(8,128)S(1)}, f32[1,128,32]{1,2,0:T(8,128)}, u32[]{:S(2)}) copy-start(f32[1,128,32]{1,2,0:T(8,128)} %param.25) | copy-start | bytes 49156
  270.5 10.2 %copy-start.2 = (bf16[1,128,2048]{2,1,0:T(8,128)(2,1)S(1)}, bf16[1,128,2048]{2,1,0:T(8,128)(2,1)}, u32[]{:S(2)}) copy-start(bf16[1,128,2048]{2,1,0:T(8,128)(2,1)} %param.14) | copy-start | bytes 1572868
  270.5 97.5 %all-to-all-start.2 = ((bf16[16,57,2048]{2,1,0:T(8,128)(2,1)}), bf16[16,57,2048]{2,1,0:T(8,128)(2,1)}, u32[]{:S(2)}, u32[]{:S(2)}) async-start(bf16[16,57,2048]{2,1,0:T(8,128)(2,1)} %reshape.336), calls=%async_computation.2 | async-start | bytes 8388608 | tf_op jit(solution)/shard_map/all_to_all | solution.py:155
  275.7 6.3 %copy-start.8 = (f32[2048]{0:T(1024)S(1)}, f32[2048]{0:T(1024)}, u32[]{:S(2)}) copy-start(f32[2048]{0:T(1024)} %param.16) | copy-start | bytes 24580
  275.7 6.4 %copy-start.11 = (f32[1,128,6]{1,0,2:T(1,128)S(1)}, f32[1,128,6]{1,0,2:T(1,128)}, u32[]{:S(2)}) copy-start(f32[1,128,6]{1,0,2:T(1,128)} %param.18) | copy-start | bytes 9220
  275.7 6.7 %copy-start.5 = (bf16[1,128,2048]{2,1,0:T(8,128)(2,1)S(1)}, bf16[1,128,2048]{2,1,0:T(8,128)(2,1)}, u32[]{:S(2)}) copy-start(bf16[1,128,2048]{2,1,0:T(8,128)(2,1)} %param.22) | copy-start | bytes 1572868
  275.7 146.3 %all-gather.4.cloned.1.call-start = ((), (), s32[]{:S(2)}) async-start(), calls=%async_computation.3 | async-start | bytes 1572864 | tf_op jit(solution)/shard_map/all_gather | solution.py:18
  280.5 3.3 copy-start.7
  280.5 3.3 copy-start.9
  282.6 89.4 %copy-start.4 = (bf16[1,128,2048]{1,2,0:T(8,128)(2,1)}, bf16[1,128,2048]{1,2,0:T(8,128)(2,1)S(1)}, u32[]{:S(2)}) copy-start(bf16[1,128,2048]{1,2,0:T(8,128)(2,1)S(1)} %copy.80) | copy-start | bytes 1572868
  400.6 2.5 copy-start.6
  427.6 7.7 %copy-start.1 = (bf16[1,2048,704]{1,2,0:T(8,128)(2,1)S(1)}, bf16[1,2048,704]{1,2,0:T(8,128)(2,1)}, u32[]{:S(2)}) copy-start(bf16[1,2048,704]{1,2,0:T(8,128)(2,1)} %param.20) | copy-start | bytes 8650756
Sparse Core Ops, SparseCore 0:
  400.8 21.2 all-gather.3
where the time goes:
time: 451 us; the launch traced here: 443 us
  waiting for transfers between devices  249 us (55%)
  local copies, waits for them, and re-layouts  88 us (20%)
  matrix products  49.7 us (11%)
  other arithmetic  19.6 us (4%)
  starting transfers between devices  17.3 us (4%)
  between operations  14.8 us (3%)
    all_to_all x1, waiting for transfers between devices, local(): lax.all_to_all(expert_result, 'exp', split_axis=0, concat_axis=0, tiled=T...  84 us
    all_to_all x1, waiting for transfers between devices, local(): lax.all_to_all(send_grads, 'exp', split_axis=0, concat_axis=0, tiled=True)  80.5 us
    all_to_all x1, waiting for transfers between devices, local(): lax.all_to_all(send_normed, 'exp', split_axis=0, concat_axis=0, tiled=True)  69 us
    dot_general x3, matrix products, transposed_product(): lax.dot_general(left_rows, weight_matrix, (((1,), (1,)), ((), ())), prefe...  28.8 us
    all_gather x1, waiting for transfers between devices, carried_in(): lax.all_gather(a.astype(kind), axis)  15.1 us
    scatter x1, local copies, waits for them, and re-layouts, local(): send_normed = jnp.zeros((expert_count * capacity, width), jnp.bfloat16).a...  10.2 us
    scatter x1, local copies, waits for them, and re-layouts, local(): send_grads = jnp.zeros((expert_count * capacity, width), jnp.bfloat16).at...  10.2 us
    gather x1, local copies, waits for them, and re-layouts, local(): expert_result.reshape(expert_count * capacity, width)[destination]  9.63 us
  transfers between devices with their start and end apart: 4, of which 4 were waited for; matrix products, arithmetic and copies ran while one was open for 10% of the time, Pallas kernels for 0%

commit v1 on v0

v1 whole, which is shorter than its diff:
```python
import functools

import jax
import jax.numpy as jnp
from jax import lax
from jax.experimental import pallas as pl
from jax.experimental.pallas import tpu as pltpu
from jax.sharding import PartitionSpec as P

TOPK = 6
EPSILON = 1e-05
BF16 = jnp.bfloat16
F32 = jnp.float32


def dot(a, b, ca, cb):
    return lax.dot_general(a, b, (((ca,), (cb,)), ((), ())), preferred_element_type=F32)


def intra_kernel(head_count, dy_ref, x_ref, key_ref, query_ref, cum_ref, cumt_ref, gx_ref, gb_ref):
    rows = dy_ref.shape[0]
    size = dy_ref.shape[1] // head_count
    pair = 128 // size
    scores = dot(key_ref[...], query_ref[...], 1, 1)
    t = lax.broadcasted_iota(jnp.int32, (rows, rows), 0)
    s = lax.broadcasted_iota(jnp.int32, (rows, rows), 1)
    later = s >= t
    lane = lax.broadcasted_iota(jnp.int32, (rows, 128), 1) // size
    mixed = jnp.zeros((rows, rows), F32)
    for p in range(head_count // pair):
        columns = slice(p * 128, (p + 1) * 128)
        dy = dy_ref[:, columns]
        x = x_ref[:, columns]
        out = jnp.zeros((rows, 128), F32)
        for q in range(pair):
            h = p * pair + q
            gap = cumt_ref[h : h + 1, :] - cum_ref[:, h : h + 1]
            decay = jnp.where(later, jnp.exp(jnp.where(later, gap, 0.0)), 0.0)
            own = lane == q
            out = jnp.where(own, dot((decay * scores).astype(BF16), dy, 1, 0), out)
            mixed = mixed + decay * dot(jnp.where(own, x, jnp.zeros_like(x)), dy, 1, 1)
        gx_ref[:, columns] = out
    gb_ref[...] = dot(mixed.astype(BF16), query_ref[...], 1, 0)


def intra_terms(dy, inputs, keys, queries, cum):
    rows, width = dy.shape
    return pl.pallas_call(
        functools.partial(intra_kernel, cum.shape[1]),
        out_shape=(
            jax.ShapeDtypeStruct((rows, width), F32),
            jax.ShapeDtypeStruct((rows, keys.shape[1]), F32),
        ),
        cost_estimate=pl.CostEstimate(flops=400_000_000, bytes_accessed=2_500_000, transcendentals=524_288),
        compiler_params=pltpu.CompilerParams(vmem_limit_bytes=24 * 1024 * 1024),
    )(dy, inputs, keys, queries, cum, cum.T)


def incoming_state(total, state):
    count = lax.axis_size("seq")
    if count == 2:
        return lax.ppermute(state.astype(BF16), "seq", [(1, 0)])
    place = lax.axis_index("seq")
    states = lax.all_gather(state.astype(BF16), "seq")
    totals = lax.all_gather(total, "seq")
    carried = jnp.zeros(state.shape, F32)
    repeat = state.shape[1] // total.shape[0]
    for block in range(count - 1, 0, -1):
        factor = jnp.repeat(jnp.exp(totals[block]), repeat)[None, :]
        joined = states[block].astype(F32) + factor * carried
        carried = jnp.where(block > place, joined, carried)
    return carried.astype(BF16)


def local(
    stream_input,
    grad_output,
    norm_gain,
    routes,
    gates,
    w_gate,
    w_up,
    w_down,
    ssd_input,
    in_keys,
    out_queries,
    log_decay,
):
    tokens = stream_input.shape[1]
    width = stream_input.shape[2]
    heads = log_decay.shape[2]
    size = width // heads
    experts = lax.axis_size("exp")
    capacity = -(-(tokens * 7 // experts + 1) // 16) * 16
    stream = stream_input[0].astype(F32)
    root = jnp.sqrt(jnp.mean(stream * stream, axis=1, keepdims=True) + EPSILON)
    unit = stream / root
    normed = (unit * norm_gain[None, :]).astype(BF16)
    grads = grad_output[0]

    names = jnp.arange(experts, dtype=jnp.int32)
    table = jnp.sum(
        jnp.where(routes[0][None] == names[:, None, None], gates[0][None], 0.0), axis=2
    )
    own_gates = lax.all_to_all(table, "exp", split_axis=0, concat_axis=0, tiled=True)
    all_normed = lax.all_gather(normed, "exp")
    all_grads = lax.all_gather(grads, "exp")

    chosen = own_gates > 0.0
    before = jnp.triu(jnp.ones((tokens, tokens), BF16), 1)
    slots = dot(chosen.astype(BF16), before, 1, 0).astype(jnp.int32)
    places = jnp.arange(capacity, dtype=jnp.int32)[None, :, None]
    picks = (slots[:, None, :] == places) & chosen[:, None, :]
    onehot = picks.astype(BF16)
    slot_gates = jnp.sum(jnp.where(picks, own_gates[:, None, :], 0.0), axis=2).reshape(-1, 1)

    def take(rows):
        taken = lax.dot_general(
            onehot, rows, (((2,), (1,)), ((0,), (0,))), preferred_element_type=F32
        )
        return taken.astype(BF16).reshape(experts * capacity, width)

    gate_weight, up_weight, down_weight = w_gate[0], w_up[0], w_down[0]
    normed_rows = take(all_normed)
    gate_pre = dot(normed_rows, gate_weight, 1, 0)
    up_pre = dot(normed_rows, up_weight, 1, 0)
    back = dot(take(all_grads), down_weight, 1, 1)
    sig = jax.nn.sigmoid(gate_pre)
    grad_gate = (back * up_pre * sig * (1.0 + gate_pre * (1.0 - sig))).astype(BF16)
    grad_up = (back * gate_pre * sig).astype(BF16)
    summed = dot(grad_gate, gate_weight, 1, 1) + dot(grad_up, up_weight, 1, 1)
    weighted = (slot_gates * summed).astype(BF16).reshape(experts, capacity, width)
    spread = lax.dot_general(
        onehot, weighted, (((1,), (1,)), ((0,), (0,))), preferred_element_type=F32
    ).astype(BF16)
    normed_grad = lax.psum_scatter(spread, "exp", scatter_dimension=0, tiled=False).astype(F32)

    scaled = normed_grad * norm_gain[None, :]
    dy = (
        grads.astype(F32)
        + (scaled - unit * jnp.mean(unit * scaled, axis=1, keepdims=True)) / root
    ).astype(BF16)

    inputs = ssd_input[0]
    keys, queries = in_keys[0], out_queries[0]
    cum = jnp.dot(
        jnp.tril(jnp.ones((tokens, tokens), F32)), log_decay[0], precision=lax.Precision.HIGHEST
    )
    total = cum[-1]
    growth = jnp.repeat(jnp.exp(cum), size, axis=1)
    edge = jnp.repeat(jnp.exp(total[None, :] - cum), size, axis=1)
    state = dot(queries, (dy.astype(F32) * growth).astype(BF16), 0, 0)
    incoming = incoming_state(total, state)
    intra_x, intra_b = intra_terms(dy, inputs, keys, queries, cum)
    grad_x = (intra_x + edge * dot(keys, incoming, 1, 0)).astype(BF16)
    grad_b = intra_b + dot((inputs.astype(F32) * edge).astype(BF16), incoming, 1, 1)
    return (dy[None], grad_x[None], grad_b[None])


def solution(mesh):
    tokens = P("exp", "seq", None)
    weights = P("exp", None, None)
    return jax.shard_map(
        local,
        mesh=mesh,
        in_specs=(tokens, tokens, P(), tokens, tokens, weights, weights, weights)
        + (tokens,) * 4,
        out_specs=(tokens,) * 3,
        check_vma=False,
    )
```

time: 451 us -> 334 us (0.74); the launches traced: 443 us -> 332 us
  local copies, waits for them, and re-layouts: 88 us -> 13.8 us
  starting transfers between devices: 17.3 us -> 1.54 us
  waiting for transfers between devices: 249 us -> 234 us
  other arithmetic: 19.6 us -> 9.14 us
  blocking collectives: 4.47 us -> 10.1 us
    all_to_all x3 -> x0, waiting for transfers between devices: 233 us -> none  [the longest x1 84 us: local(): lax.all_to_all(expert_result, 'exp', split_axis=0, concat_axis=0, tiled=T...]
    all_gather x1 -> x2, waiting for transfers between devices: 15.1 us -> 126 us  [the longest x1 63.9 us: local(): all_grads = lax.all_gather(grads, 'exp')]
    reduce_scatter x0 -> x1, waiting for transfers between devices: none -> 96.3 us  [local(): lax.psum_scatter(spread, 'exp', scatter_dimension=0, tiled=False)]
    reshape x9 -> x1, local copies, waits for them, and re-layouts: 37.1 us -> 2.61 us  [local(): edge = jnp.repeat(jnp.exp(total[None, :] - cum), size, axis=1)]
    scatter x2 -> x0, local copies, waits for them, and re-layouts: 20.3 us -> none  [the longest x1 10.2 us: local(): send_normed = jnp.zeros((expert_count * capacity, width), jnp.bfloat16).a...]
    all_to_all x3 -> x0, starting transfers between devices: 17.3 us -> none  [the longest x1 6.69 us: local(): lax.all_to_all(send_normed, 'exp', split_axis=0, concat_axis=0, tiled=True)]
    ppermute x0 -> x1, waiting for transfers between devices: none -> 10.9 us  [incoming_state(): return lax.ppermute(state.astype(BF16), 'seq', [(1, 0)])]
    all_to_all x0 -> x1, blocking collectives: none -> 10.1 us  [local(): lax.all_to_all(table, 'exp', split_axis=0, concat_axis=0, tiled=True)]
  transfers between devices with their start and end apart: 4 -> 4, of which waited for: 4 -> 4; matrix products, arithmetic and copies ran while one was open for 10% -> 6% of each run, Pallas kernels for 0% -> 0%
where the time goes in v1:
time: 334 us; the launch traced here: 332 us
  waiting for transfers between devices  234 us (70%)
  matrix products  48.6 us (15%)
  between operations  13.9 us (4%)
  local copies, waits for them, and re-layouts  13.8 us (4%)
  blocking collectives  10.1 us (3%)
  other arithmetic  9.14 us (3%)
    reduce_scatter x1, waiting for transfers between devices, local(): lax.psum_scatter(spread, 'exp', scatter_dimension=0, tiled=False)  96.3 us
    all_gather x1, waiting for transfers between devices, local(): all_grads = lax.all_gather(grads, 'exp')  63.9 us
    all_gather x1, waiting for transfers between devices, local(): all_normed = lax.all_gather(normed, 'exp')  61.9 us
    dot_general x8, matrix products, dot(): lax.dot_general(a, b, (((ca,), (cb,)), ((), ())), preferred_element_type=...  33.3 us
    ppermute x1, waiting for transfers between devices, incoming_state(): return lax.ppermute(state.astype(BF16), 'seq', [(1, 0)])  10.9 us
    all_to_all x1, blocking collectives, local(): lax.all_to_all(table, 'exp', split_axis=0, concat_axis=0, tiled=True)  10.1 us
    dot_general x2, matrix products, take(): lax.dot_general(onehot, rows, (((2,), (1,)), ((0,), (0,))), preferred_ele...  9.54 us
  transfers between devices with their start and end apart: 4, of which 4 were waited for; matrix products, arithmetic and copies ran while one was open for 6% of the time, Pallas kernels for 0%

profile of v1, /device:TPU:10, one launch (start us, length us, event | category | flops | bytes accessed | tf_op | source)
XLA Modules:
  0.0 332.4 jit_solution(4890653909787394383)
XLA Ops:
  7.2 0.0 copy-start
  7.2 0.0 all-gather.5.cloned.1.call-start
  7.2 1.4 fusion.19
  8.6 2.0 multiply_convert_fusion.6
  10.7 0.0 all-gather.5.cloned.1.call-update
  10.7 0.0 all-gather.3.cloned.1.call-start
  10.7 0.7 all-gather.3.cloned.1.call-update
  11.4 0.0 reduce-scatter.2.cloned.1.call-start
  11.5 0.7 copy.63
  12.2 0.7 copy.64
  12.9 10.1 %all_to_all.12 = f32[16,1,128]{2,1,0:T(1,128)S(1)} all-to-all(f32[16,1,128]{2,1,0:T(1,128)S(1)} %bitcast.113), channel_id=1, replica_groups=mesh['seq'=2,'exp'=16] {'exp'}, dimensions={0} | all-to-all | bytes 16384 | tf_op jit(solution)/shard_map/all_to_all | solution.py:105
  23.0 0.1 convolution_convert_fusion.4
  23.1 0.2 select_reduce_fusion
  23.4 0.1 mul.107
  23.5 61.9 %all-gather.5.cloned.1.call-done = bf16[16,128,2048]{2,1,0:T(8,128)(2,1)} async-done(((bf16[1,128,2048]{2,1,0:T(8,128)(2,1)}), bf16[16,128,2048]{2,1,0:T(8,128)(2,1)}) %all-gather.5.cloned.1.call-update) | async-done | bytes 8388624 | tf_op jit(solution)/shard_map/all_gather | solution.py:106
  85.4 4.8 %convolution_convert_fusion.1 = bf16[16,64,2048]{2,1,0:T(8,128)(2,1)S(1)} fusion(bf16[16,128,2048]{2,1,0:T(8,128)(2,1)} %all-gather.5.cloned.1.call-done, s32[16,128]{1,0:T(8,128)S(1)} %convolution_convert_fusion.4, pred[16,128]{1,0:T(8,128)(4,1)S(1)} %compare_bitcast_fusion), kind=kOutput, calls=%fused_computation.2 | convolution fusion | flops 539230208 | bytes 12593152 | tf_op jit(solution)/shard_map/dot_general | solution.py:118
  90.2 2.0 copy-done.5
  92.1 4.7 %fusion.2 = f32[1024,704]{0,1:T(8,128)} fusion(bf16[1024,2048]{1,0:T(8,128)(2,1)S(1)} %bitcast.101, bf16[1,2048,704]{1,2,0:T(8,128)(2,1)S(1)} %copy-done.11), kind=kOutput, calls=%fused_computation.6 | convolution fusion | flops 2952790016 | bytes 9961472 | tf_op jit(solution)/shard_map/dot_general | solution.py:17
  96.9 63.9 %all-gather.3.cloned.1.call-done = bf16[16,128,2048]{2,1,0:T(8,128)(2,1)} async-done(((bf16[1,128,2048]{2,1,0:T(8,128)(2,1)}), bf16[16,128,2048]{2,1,0:T(8,128)(2,1)}) %all-gather.3.cloned.1.call-update) | async-done | bytes 8388624 | tf_op jit(solution)/shard_map/all_gather | solution.py:107
  160.7 4.8 %convolution_convert_fusion.2 = bf16[16,64,2048]{2,1,0:T(8,128)(2,1)S(1)} fusion(bf16[16,128,2048]{2,1,0:T(8,128)(2,1)} %all-gather.3.cloned.1.call-done, s32[16,128]{1,0:T(8,128)S(1)} %convolution_convert_fusion.4, pred[16,128]{1,0:T(8,128)(4,1)S(1)} %compare_bitcast_fusion), kind=kOutput, calls=%fused_computation.3 | convolution fusion | flops 539230208 | bytes 12593152 | tf_op jit(solution)/shard_map/dot_general | solution.py:118
  165.5 4.7 %fusion.7 = f32[1024,704]{0,1:T(8,128)} fusion(bf16[1024,2048]{1,0:T(8,128)(2,1)S(1)} %bitcast.103, bf16[1,704,2048]{2,1,0:T(8,128)(2,1)S(1)} %copy-done.10), kind=kOutput, calls=%fused_computation.11 | convolution fusion | flops 2952790016 | bytes 9961472 | tf_op jit(solution)/shard_map/dot_general | solution.py:17
  170.2 13.6 %fusion = f32[1024,2048]{1,0:T(8,128)} fusion(bf16[1,2048,704]{1,2,0:T(8,128)(2,1)} %param.17, f32[1024,704]{0,1:T(8,128)} %fusion.2, f32[1024,704]{0,1:T(8,128)} %fusion.7, bf16[1024,2048]{1,0:T(8,128)(2,1)} %bitcast.102, bf16[1,2048,704]{1,2,0:T(8,128)(2,1)S(1)} %copy-done), kind=kOutput, calls=%fused_computation.4 | convolution fusion | flops 5912788992 | bytes 24117248 | tf_op jit(solution)/shard_map/dot_general | solution.py:17
  183.8 7.7 %multiply_convert_fusion = bf16[1024,2048]{1,0:T(8,128)(2,1)S(1)} fusion(f32[1024,2048]{1,0:T(8,128)} %fusion, f32[1024]{0:T(1024)S(1)} %mul.107, bf16[1,2048,704]{1,2,0:T(8,128)(2,1)S(1)} %copy-done, f32[1024,704]{0,1:T(8,128)} %fusion.7, f32[1024,704]{0,1:T(8,128)} %fusion.2), kind=kOutput, calls=%fused_computation | convolution fusion | flops 2963406848 | bytes 21237760 | tf_op jit(solution)/shard_map/dot_general | solution.py:17
  191.6 5.6 %convolution_convert_fusion = bf16[16,128,2048]{2,1,0:T(8,128)(2,1)} fusion(bf16[16,64,2048]{2,1,0:T(8,128)(2,1)S(1)} %bitcast.104, s32[16,128]{1,0:T(8,128)S(1)} %convolution_convert_fusion.4, pred[16,128]{1,0:T(8,128)(4,1)S(1)} %compare_bitcast_fusion), kind=kOutput, calls=%fused_computation.1 | convolution fusion | flops 541327360 | bytes 12593152 | tf_op jit(solution)/shard_map/dot_general | solution.py:133
  197.2 0.0 reduce-scatter.2.cloned.1.call-update
  197.2 0.0 copy-start.9
  197.2 0.0 copy-start.12
  197.3 2.3 copy.52
  199.5 1.2 copy.54
  200.7 0.7 mul.127
  201.4 0.2 fusion.32
  201.6 0.1 copy.51.cum_ref
  201.7 0.2 slice_reduce_fusion
  201.9 0.1 fusion.53
  202.0 1.1 broadcast_in_dim.71
  203.1 2.6 copy.56
  205.7 96.3 %reduce-scatter.2.cloned.1.call-done = bf16[1,128,2048]{2,1,0:T(8,128)(2,1)} async-done(((bf16[16,128,2048]{2,1,0:T(8,128)(2,1)}), bf16[1,128,2048]{2,1,0:T(8,128)(2,1)}) %reduce-scatter.2.cloned.1.call-update) | async-done | bytes 524304 | tf_op jit(solution)/shard_map/reduce_scatter | solution.py:136
  302.0 1.4 multiply_reduce_fusion
  303.3 2.2 copy.53
  305.6 2.4 multiply_convert_fusion.5
  308.0 0.3 fusion.12
  308.3 1.4 collective-permute-start
  309.8 0.4 fusion.18.dy_ref
  310.2 1.6 shard_map.139
  311.8 1.2 add_convert_fusion.1
  313.0 10.9 %collective-permute-done = bf16[128,2048]{0,1:T(8,128)(2,1)S(1)} collective-permute-done((bf16[128,2048]{0,1:T(8,128)(2,1)S(1)}, bf16[128,2048]{0,1:T(8,128)(2,1)S(1)}, u32[]{:S(2)}, u32[]{:S(2)}) %collective-permute-start) | collective-permute-done | bytes 524320 | tf_op jit(solution)/shard_map/ppermute | solution.py:62
  323.9 0.9 fusion.17
  324.8 1.1 fusion.13
  (26 shorter events, 0.1 us)
Async XLA Ops:
  7.2 163.1 %copy-start = (bf16[1,2048,704]{1,2,0:T(8,128)(2,1)S(1)}, bf16[1,2048,704]{1,2,0:T(8,128)(2,1)}, u32[]{:S(2)}) copy-start(bf16[1,2048,704]{1,2,0:T(8,128)(2,1)} %param.18) | copy-start | bytes 8650756
  7.2 78.2 %all-gather.5.cloned.1.call-start = ((), (), s32[]{:S(2)}) async-start(), calls=%async_computation.3 | async-start | bytes 8912896 | tf_op jit(solution)/shard_map/all_gather | solution.py:106
  10.7 150.0 %all-gather.3.cloned.1.call-start = ((), (), s32[]{:S(2)}) async-start(), calls=%async_computation.2 | async-start | bytes 8912896 | tf_op jit(solution)/shard_map/all_gather | solution.py:107
  11.4 290.5 %reduce-scatter.2.cloned.1.call-start = ((), (), s32[]{:S(2)}) async-start(), calls=%async_computation.4 | async-start | bytes 8912896 | tf_op jit(solution)/shard_map/reduce_scatter | solution.py:136
  85.4 6.7 %copy-start.11 = (bf16[1,2048,704]{1,2,0:T(8,128)(2,1)S(1)}, bf16[1,2048,704]{1,2,0:T(8,128)(2,1)}, u32[]{:S(2)}) copy-start(bf16[1,2048,704]{1,2,0:T(8,128)(2,1)} %param.17) | copy-start | bytes 8650756
  90.1 2.0 copy-start.5
  160.7 4.8 %copy-start.10 = (bf16[1,704,2048]{2,1,0:T(8,128)(2,1)S(1)}, bf16[1,704,2048]{2,1,0:T(8,128)(2,1)}, u32[]{:S(2)}) copy-start(bf16[1,704,2048]{2,1,0:T(8,128)(2,1)} %param.19) | copy-start | bytes 8650756
  197.2 2.3 copy-start.4
  197.2 3.5 %copy-start.9 = (f32[2048]{0:T(1024)S(1)}, f32[2048]{0:T(1024)}, u32[]{:S(2)}) copy-start(f32[2048]{0:T(1024)} %param.14) | copy-start | bytes 24580
  197.2 4.1 %copy-start.12 = (f32[1,128,32]{1,2,0:T(8,128)S(1)}, f32[1,128,32]{1,2,0:T(8,128)}, u32[]{:S(2)}) copy-start(f32[1,128,32]{1,2,0:T(8,128)} %param.23) | copy-start | bytes 49156
  303.3 4.7 %copy-start.3 = (bf16[1,128,128]{2,1,0:T(8,128)(2,1)S(1)}, bf16[1,128,128]{2,1,0:T(8,128)(2,1)}, u32[]{:S(2)}) copy-start(bf16[1,128,128]{2,1,0:T(8,128)(2,1)} %param.22) | copy-start | bytes 98308
  305.6 4.2 %copy-start.7 = (bf16[1,128,2048]{2,1,0:T(8,128)(2,1)S(1)}, bf16[1,128,2048]{2,1,0:T(8,128)(2,1)}, u32[]{:S(2)}) copy-start(bf16[1,128,2048]{2,1,0:T(8,128)(2,1)} %param.13) | copy-start | bytes 1572868
  305.6 4.2 %copy-start.8 = (bf16[1,128,2048]{2,1,0:T(8,128)(2,1)S(1)}, bf16[1,128,2048]{2,1,0:T(8,128)(2,1)}, u32[]{:S(2)}) copy-start(bf16[1,128,2048]{2,1,0:T(8,128)(2,1)} %reduce-scatter.2.cloned.1.call-done) | copy-start | bytes 1572868
  305.6 4.6 %copy-start.1 = (bf16[1,128,2048]{2,1,0:T(8,128)(2,1)S(1)}, bf16[1,128,2048]{2,1,0:T(8,128)(2,1)}, u32[]{:S(2)}) copy-start(bf16[1,128,2048]{2,1,0:T(8,128)(2,1)} %param.20) | copy-start | bytes 1572868
  305.6 4.6 %copy-start.2 = (bf16[1,128,128]{2,1,0:T(8,128)(2,1)S(1)}, bf16[1,128,128]{2,1,0:T(8,128)(2,1)}, u32[]{:S(2)}) copy-start(bf16[1,128,128]{2,1,0:T(8,128)(2,1)} %param.21) | copy-start | bytes 98308
  308.3 15.5 %copy-start.6 = (f32[128,2048]{1,0:T(8,128)S(1)}, f32[128,2048]{1,0:T(8,128)}, u32[]{:S(2)}) copy-start(f32[128,2048]{1,0:T(8,128)} %copy.56) | copy-start | bytes 3145732
  308.3 15.5 %collective-permute-start = (bf16[128,2048]{0,1:T(8,128)(2,1)S(1)}, bf16[128,2048]{0,1:T(8,128)(2,1)S(1)}, u32[]{:S(2)}, u32[]{:S(2)}) collective-permute-start(bf16[128,2048]{0,1:T(8,128)(2,1)S(1)} %fusion.12), channel_id=1, source_target_pairs={{16,0},{17,1},{18,2},{19,3},{20,4},{21,5},{22,6},{23,7},{24,8},{25... | collective-permute-start | bytes 1572872 | tf_op jit(solution)/shard_map/ppermute | solution.py:62
Sparse Core Ops, SparseCore 0:
  10.8 74.5 all-gather.4
  87.5 73.1 all-gather.2
  197.4 104.5 reduce-scatter.1

commit v2 on v1

--- a/solution.py
+++ b/solution.py
@@ -128,12 +128,17 @@
     sig = jax.nn.sigmoid(gate_pre)
     grad_gate = (back * up_pre * sig * (1.0 + gate_pre * (1.0 - sig))).astype(BF16)
     grad_up = (back * gate_pre * sig).astype(BF16)
-    summed = dot(grad_gate, gate_weight, 1, 1) + dot(grad_up, up_weight, 1, 1)
-    weighted = (slot_gates * summed).astype(BF16).reshape(experts, capacity, width)
-    spread = lax.dot_general(
-        onehot, weighted, (((1,), (1,)), ((0,), (0,))), preferred_element_type=F32
-    ).astype(BF16)
-    normed_grad = lax.psum_scatter(spread, "exp", scatter_dimension=0, tiled=False).astype(F32)
+    half = width // 2
+    parts = []
+    for first in (0, half):
+        rows = slice(first, first + half)
+        summed = dot(grad_gate, gate_weight[rows], 1, 1) + dot(grad_up, up_weight[rows], 1, 1)
+        weighted = (slot_gates * summed).astype(BF16).reshape(experts, capacity, half)
+        spread = lax.dot_general(
+            onehot, weighted, (((1,), (1,)), ((0,), (0,))), preferred_element_type=F32
+        ).astype(BF16)
+        parts.append(lax.psum_scatter(spread, "exp", scatter_dimension=0, tiled=False))
+    normed_grad = jnp.concatenate(parts, axis=1).astype(F32)
 
     scaled = normed_grad * norm_gain[None, :]
     dy = (

time: 334 us -> 361 us (1.081)
  waiting for transfers between devices: 234 us -> 267 us
  matrix products: 48.6 us -> 40.3 us
    reduce_scatter x1 -> x2, waiting for transfers between devices: 96.3 us -> 131 us  [local(): lax.psum_scatter(spread, 'exp', scatter_dimension=0, tiled=False)]
    dot_general x8 -> x11, matrix products: 33.3 us -> 24 us  [dot(): lax.dot_general(a, b, (((ca,), (cb,)), ((), ())), preferred_element_type=...]
  transfers between devices with their start and end apart: 4 -> 5, of which waited for: 4 -> 5; matrix products, arithmetic and copies ran while one was open for 6% -> 8% of each run, Pallas kernels for 0% -> 0%
where the time goes in v2:
time: 361 us; the launch traced here: 358 us
  waiting for transfers between devices  267 us (74%)
  matrix products  40.3 us (11%)
  between operations  14.2 us (4%)
  local copies, waits for them, and re-layouts  14 us (4%)
  blocking collectives  10.1 us (3%)
  other arithmetic  9.5 us (3%)
    reduce_scatter x2, waiting for transfers between devices, local(): lax.psum_scatter(spread, 'exp', scatter_dimension=0, tiled=False)  131 us
    all_gather x1, waiting for transfers between devices, local(): all_grads = lax.all_gather(grads, 'exp')  63.8 us
    all_gather x1, waiting for transfers between devices, local(): all_normed = lax.all_gather(normed, 'exp')  61.9 us
    dot_general x11, matrix products, dot(): lax.dot_general(a, b, (((ca,), (cb,)), ((), ())), preferred_element_type=...  24 us
    all_to_all x1, blocking collectives, local(): lax.all_to_all(table, 'exp', split_axis=0, concat_axis=0, tiled=True)  10.1 us
    ppermute x1, waiting for transfers between devices, incoming_state(): return lax.ppermute(state.astype(BF16), 'seq', [(1, 0)])  9.77 us
    dot_general x2, matrix products, take(): lax.dot_general(onehot, rows, (((2,), (1,)), ((0,), (0,))), preferred_ele...  9.54 us
  transfers between devices with their start and end apart: 5, of which 5 were waited for; matrix products, arithmetic and copies ran while one was open for 8% of the time, Pallas kernels for 0%

profile of v2, /device:TPU:10, one launch (start us, length us, event | category | flops | bytes accessed | tf_op | source)
XLA Modules:
  0.0 358.3 jit_solution(8809339055140367305)
XLA Ops:
  7.2 1.4 fusion.25
  8.6 2.0 multiply_convert_fusion.6
  10.7 0.7 all-gather.3.cloned.1.call-update
  11.5 0.7 copy.68
  12.2 0.7 copy.67
  12.9 10.1 %all_to_all.12 = f32[16,1,128]{2,1,0:T(1,128)S(1)} all-to-all(f32[16,1,128]{2,1,0:T(1,128)S(1)} %bitcast.130), channel_id=1, replica_groups=mesh['seq'=2,'exp'=16] {'exp'}, dimensions={0} | all-to-all | bytes 16384 | tf_op jit(solution)/shard_map/all_to_all | solution.py:105
  23.0 0.1 convolution_convert_fusion.5
  23.1 0.2 select_reduce_fusion
  23.4 0.1 mul.119
  23.5 61.9 %all-gather.5.cloned.1.call-done = bf16[16,128,2048]{2,1,0:T(8,128)(2,1)} async-done(((bf16[1,128,2048]{2,1,0:T(8,128)(2,1)}), bf16[16,128,2048]{2,1,0:T(8,128)(2,1)}) %all-gather.5.cloned.1.call-update) | async-done | bytes 8388624 | tf_op jit(solution)/shard_map/all_gather | solution.py:106
  85.4 4.8 %convolution_convert_fusion = bf16[16,64,2048]{2,1,0:T(8,128)(2,1)S(1)} fusion(bf16[16,128,2048]{2,1,0:T(8,128)(2,1)} %all-gather.5.cloned.1.call-done, s32[16,128]{1,0:T(8,128)S(1)} %convolution_convert_fusion.5, pred[16,128]{1,0:T(8,128)(4,1)S(1)} %compare_bitcast_fusion), kind=kOutput, calls=%fused_computation.2 | convolution fusion | flops 539230208 | bytes 12593152 | tf_op jit(solution)/shard_map/dot_general | solution.py:118
  90.2 2.0 copy-done.7
  92.1 4.7 %fusion = f32[1024,704]{0,1:T(8,128)} fusion(bf16[1024,2048]{1,0:T(8,128)(2,1)S(1)} %bitcast.112, bf16[1,2048,704]{1,2,0:T(8,128)(2,1)S(1)} %copy-done.15), kind=kOutput, calls=%fused_computation.4 | convolution fusion | flops 2952790016 | bytes 9961472 | tf_op jit(solution)/shard_map/dot_general | solution.py:17
  96.9 63.8 %all-gather.3.cloned.1.call-done = bf16[16,128,2048]{2,1,0:T(8,128)(2,1)} async-done(((bf16[1,128,2048]{2,1,0:T(8,128)(2,1)}), bf16[16,128,2048]{2,1,0:T(8,128)(2,1)}) %all-gather.3.cloned.1.call-update) | async-done | bytes 8388624 | tf_op jit(solution)/shard_map/all_gather | solution.py:107
  160.7 4.8 %convolution_convert_fusion.1 = bf16[16,64,2048]{2,1,0:T(8,128)(2,1)S(1)} fusion(bf16[16,128,2048]{2,1,0:T(8,128)(2,1)} %all-gather.3.cloned.1.call-done, s32[16,128]{1,0:T(8,128)S(1)} %convolution_convert_fusion.5, pred[16,128]{1,0:T(8,128)(4,1)S(1)} %compare_bitcast_fusion), kind=kOutput, calls=%fused_computation.3 | convolution fusion | flops 539230208 | bytes 12593152 | tf_op jit(solution)/shard_map/dot_general | solution.py:118
  165.5 3.5 multiply_convert_fusion.2
  169.1 3.9 %multiply_convert_fusion.3 = bf16[1024,704]{0,1:T(8,128)(2,1)S(1)} fusion(f32[1024,704]{0,1:T(8,128)S(1)} %copy-done.24, f32[1024,704]{0,1:T(8,128)S(1)} %get-tuple-element.10, bf16[1024,2048]{1,0:T(8,128)(2,1)S(1)} %bitcast.113, bf16[1,2048,704]{1,2,0:T(8,128)(2,1)S(1)} %copy-done.18), kind=kOutput, calls=%fused_computation.11 | convolution fusion | flops 2959998976 | bytes 14286848 | tf_op jit(solution)/shard_map/dot_general | solution.py:17
  173.0 2.1 fusion.14
  175.1 2.0 multiply_convert_fusion
  177.1 3.2 convolution_convert_fusion.2
  180.4 1.7 copy-done.17
  182.2 3.4 fusion.17
  185.6 2.0 multiply_convert_fusion.1
  187.6 3.3 convolution_convert_fusion.3
  190.9 0.7 copy-done.14
  191.6 0.3 copy-done.10
  191.9 0.2 copy.55
  192.1 1.2 copy.58
  193.3 0.2 fusion.39
  193.5 0.1 copy.54.cum_ref
  193.7 0.2 slice_reduce_fusion
  193.8 0.1 fusion.58
  193.9 1.1 broadcast_in_dim.71
  195.0 2.7 copy.60
  197.7 54.8 %reduce-scatter.5.cloned.1.call-done = bf16[1,128,1024]{2,1,0:T(8,128)(2,1)} async-done(((bf16[16,128,1024]{2,1,0:T(8,128)(2,1)}), bf16[1,128,1024]{2,1,0:T(8,128)(2,1)}) %reduce-scatter.5.cloned.1.call-update) | async-done | bytes 262160 | tf_op jit(solution)/shard_map/reduce_scatter | solution.py:140
  252.4 76.0 %reduce-scatter.3.cloned.1.call-done = bf16[1,128,1024]{2,1,0:T(8,128)(2,1)} async-done(((bf16[16,128,1024]{2,1,0:T(8,128)(2,1)}), bf16[1,128,1024]{2,1,0:T(8,128)(2,1)}) %reduce-scatter.3.cloned.1.call-update) | async-done | bytes 262160 | tf_op jit(solution)/shard_map/reduce_scatter | solution.py:140
  328.4 1.3 multiply_reduce_fusion
  329.8 1.4 fusion.24.dy_ref
  331.2 1.2 copy.57
  332.4 1.1 copy.56
  333.6 1.8 multiply_convert_fusion.5
  335.4 0.3 fusion.9
  335.7 1.4 collective-permute-start
  337.1 1.6 shard_map.139
  338.8 1.2 add_convert_fusion.1
  339.9 9.8 %collective-permute-done = bf16[128,2048]{0,1:T(8,128)(2,1)S(1)} collective-permute-done((bf16[128,2048]{0,1:T(8,128)(2,1)S(1)}, bf16[128,2048]{0,1:T(8,128)(2,1)S(1)}, u32[]{:S(2)}, u32[]{:S(2)}) %collective-permute-start) | collective-permute-done | bytes 524320 | tf_op jit(solution)/shard_map/ppermute | solution.py:62
  349.7 1.1 fusion.10
  350.8 0.9 fusion.23
  (58 shorter events, 0.4 us)
Async XLA Ops:
  7.2 158.3 %copy-start = (bf16[1,704,2048]{2,1,0:T(8,128)(2,1)S(1)}, bf16[1,704,2048]{2,1,0:T(8,128)(2,1)}, u32[]{:S(2)}) copy-start(bf16[1,704,2048]{2,1,0:T(8,128)(2,1)} %param.19) | copy-start | bytes 8650756
  7.2 78.2 %all-gather.5.cloned.1.call-start = ((), (), s32[]{:S(2)}) async-start(), calls=%async_computation.4 | async-start | bytes 8912896 | tf_op jit(solution)/shard_map/all_gather | solution.py:106
  10.7 150.0 %all-gather.3.cloned.1.call-start = ((), (), s32[]{:S(2)}) async-start(), calls=%async_computation.3 | async-start | bytes 8912896 | tf_op jit(solution)/shard_map/all_gather | solution.py:107
  11.4 241.0 %reduce-scatter.5.cloned.1.call-start = ((), (), s32[]{:S(2)}) async-start(), calls=%async_computation.6 | async-start | bytes 4456448 | tf_op jit(solution)/shard_map/reduce_scatter | solution.py:140
  85.4 6.8 %copy-start.15 = (bf16[1,2048,704]{1,2,0:T(8,128)(2,1)S(1)}, bf16[1,2048,704]{1,2,0:T(8,128)(2,1)}, u32[]{:S(2)}) copy-start(bf16[1,2048,704]{1,2,0:T(8,128)(2,1)} %param.17) | copy-start | bytes 8650756
  90.1 2.0 copy-start.7
  160.7 4.8 %copy-start.24 = (f32[1024,704]{0,1:T(8,128)S(1)}, f32[1024,704]{0,1:T(8,128)}, u32[]{:S(2)}) copy-start(f32[1024,704]{0,1:T(8,128)} %fusion) | copy-start | bytes 8650756
  165.5 3.6 copy-start.8
  165.5 3.6 copy-start.18
  169.1 6.0 %copy-start.22 = (bf16[1024,704]{0,1:T(8,128)(2,1)}, bf16[1024,704]{0,1:T(8,128)(2,1)S(1)}, u32[]{:S(2)}) copy-start(bf16[1024,704]{0,1:T(8,128)(2,1)S(1)} %get-tuple-element.9) | copy-start | bytes 4325380
  169.1 3.9 %copy-start.16 = (bf16[1,2048,704]{1,2,0:T(8,128)(2,1)S(1)}, bf16[1,2048,704]{1,2,0:T(8,128)(2,1)}, u32[]{:S(2)}) copy-start(bf16[1,2048,704]{1,2,0:T(8,128)(2,1)} %param.17) | copy-start | bytes 8650756
  173.0 2.1 copy-start.21
  180.3 1.8 copy-start.17
  180.4 148.0 %reduce-scatter.3.cloned.1.call-start = ((), (), s32[]{:S(2)}) async-start(), calls=%async_computation.5 | async-start | bytes 4456448 | tf_op jit(solution)/shard_map/reduce_scatter | solution.py:140
  182.2 3.4 copy-start.19
  182.2 3.4 copy-start.23
  190.8 0.7 copy-start.14
  190.8 1.1 copy-start.10
  190.8 1.3 copy-start.5
  190.8 2.5 copy-start.20
  329.8 5.6 %copy-start.4 = (bf16[1,128,128]{2,1,0:T(8,128)(2,1)S(1)}, bf16[1,128,128]{2,1,0:T(8,128)(2,1)}, u32[]{:S(2)}) copy-start(bf16[1,128,128]{2,1,0:T(8,128)(2,1)} %param.22) | copy-start | bytes 98308
  331.2 5.9 %copy-start.2 = (bf16[1,128,2048]{2,1,0:T(8,128)(2,1)S(1)}, bf16[1,128,2048]{2,1,0:T(8,128)(2,1)}, u32[]{:S(2)}) copy-start(bf16[1,128,2048]{2,1,0:T(8,128)(2,1)} %param.20) | copy-start | bytes 1572868
  331.2 5.9 %copy-start.3 = (bf16[1,128,128]{2,1,0:T(8,128)(2,1)S(1)}, bf16[1,128,128]{2,1,0:T(8,128)(2,1)}, u32[]{:S(2)}) copy-start(bf16[1,128,128]{2,1,0:T(8,128)(2,1)} %param.21) | copy-start | bytes 98308
  333.5 5.2 %copy-start.6 = (bf16[1,128,2048]{2,1,0:T(8,128)(2,1)S(1)}, bf16[1,128,2048]{2,1,0:T(8,128)(2,1)}, u32[]{:S(2)}) copy-start(bf16[1,128,2048]{2,1,0:T(8,128)(2,1)} %param.12) | copy-start | bytes 1572868
  333.6 5.2 %copy-start.11 = (bf16[1,128,2048]{2,1,0:T(8,128)(2,1)S(1)}, bf16[1,128,2048]{2,1,0:T(8,128)(2,1)}, u32[]{:S(2)}) copy-start(bf16[1,128,2048]{2,1,0:T(8,128)(2,1)} %param.13) | copy-start | bytes 1572868
  333.6 5.2 %copy-start.12 = (bf16[1,128,1024]{2,1,0:T(8,128)(2,1)S(1)}, bf16[1,128,1024]{2,1,0:T(8,128)(2,1)}, u32[]{:S(2)}) copy-start(bf16[1,128,1024]{2,1,0:T(8,128)(2,1)} %reduce-scatter.5.cloned.1.call-done) | copy-start | bytes 786436
  333.6 5.2 %copy-start.13 = (bf16[1,128,1024]{2,1,0:T(8,128)(2,1)S(1)}, bf16[1,128,1024]{2,1,0:T(8,128)(2,1)}, u32[]{:S(2)}) copy-start(bf16[1,128,1024]{2,1,0:T(8,128)(2,1)} %reduce-scatter.3.cloned.1.call-done) | copy-start | bytes 786436
  335.4 14.3 %copy-start.9 = (f32[128,2048]{1,0:T(8,128)S(1)}, f32[128,2048]{1,0:T(8,128)}, u32[]{:S(2)}) copy-start(f32[128,2048]{1,0:T(8,128)} %copy.60) | copy-start | bytes 3145732
  335.7 14.0 %collective-permute-start = (bf16[128,2048]{0,1:T(8,128)(2,1)S(1)}, bf16[128,2048]{0,1:T(8,128)(2,1)S(1)}, u32[]{:S(2)}, u32[]{:S(2)}) collective-permute-start(bf16[128,2048]{0,1:T(8,128)(2,1)S(1)} %fusion.9), channel_id=1, source_target_pairs={{16,0},{17,1},{18,2},{19,3},{20,4},{21,5},{22,6},{23,7},{24,8},{25... | collective-permute-start | bytes 1572872 | tf_op jit(solution)/shard_map/ppermute | solution.py:62
  338.7 13.0 %copy-start.1 = (bf16[1,704,2048]{2,1,0:T(8,128)(2,1)S(1)}, bf16[1,704,2048]{2,1,0:T(8,128)(2,1)}, u32[]{:S(2)}) copy-start(bf16[1,704,2048]{2,1,0:T(8,128)(2,1)} %param.19) | copy-start | bytes 8650756
Sparse Core Ops, SparseCore 0:
  10.8 74.5 all-gather.4
  87.5 73.1 all-gather.2
  180.5 71.9 reduce-scatter.4
  256.7 71.7 reduce-scatter.2

commit v3 on v1

--- a/solution.py
+++ b/solution.py
@@ -104,36 +104,40 @@
     )
     own_gates = lax.all_to_all(table, "exp", split_axis=0, concat_axis=0, tiled=True)
     all_normed = lax.all_gather(normed, "exp")
-    all_grads = lax.all_gather(grads, "exp")
 
-    chosen = own_gates > 0.0
     before = jnp.triu(jnp.ones((tokens, tokens), BF16), 1)
-    slots = dot(chosen.astype(BF16), before, 1, 0).astype(jnp.int32)
     places = jnp.arange(capacity, dtype=jnp.int32)[None, :, None]
-    picks = (slots[:, None, :] == places) & chosen[:, None, :]
-    onehot = picks.astype(BF16)
-    slot_gates = jnp.sum(jnp.where(picks, own_gates[:, None, :], 0.0), axis=2).reshape(-1, 1)
 
-    def take(rows):
-        taken = lax.dot_general(
-            onehot, rows, (((2,), (1,)), ((0,), (0,))), preferred_element_type=F32
+    def picks(weights):
+        chosen = weights > 0.0
+        slots = dot(chosen.astype(BF16), before, 1, 0).astype(jnp.int32)
+        return (slots[:, None, :] == places) & chosen[:, None, :]
+
+    sent = picks(table).astype(BF16).reshape(experts * capacity, tokens)
+    send_grads = dot(sent, grads, 1, 0).astype(BF16).reshape(experts, capacity, width)
+    grad_rows = lax.all_to_all(send_grads, "exp", split_axis=0, concat_axis=0, tiled=True)
+    grad_rows = grad_rows.reshape(experts * capacity, width)
+
+    held = picks(own_gates)
+    slot_gates = jnp.sum(jnp.where(held, own_gates[:, None, :], 0.0), axis=2).reshape(-1, 1)
+    normed_rows = (
+        lax.dot_general(
+            held.astype(BF16), all_normed, (((2,), (1,)), ((0,), (0,))), preferred_element_type=F32
         )
-        return taken.astype(BF16).reshape(experts * capacity, width)
-
+        .astype(BF16)
+        .reshape(experts * capacity, width)
+    )
     gate_weight, up_weight, down_weight = w_gate[0], w_up[0], w_down[0]
-    normed_rows = take(all_normed)
+    back = dot(grad_rows, down_weight, 1, 1)
     gate_pre = dot(normed_rows, gate_weight, 1, 0)
     up_pre = dot(normed_rows, up_weight, 1, 0)
-    back = dot(take(all_grads), down_weight, 1, 1)
     sig = jax.nn.sigmoid(gate_pre)
     grad_gate = (back * up_pre * sig * (1.0 + gate_pre * (1.0 - sig))).astype(BF16)
     grad_up = (back * gate_pre * sig).astype(BF16)
     summed = dot(grad_gate, gate_weight, 1, 1) + dot(grad_up, up_weight, 1, 1)
     weighted = (slot_gates * summed).astype(BF16).reshape(experts, capacity, width)
-    spread = lax.dot_general(
-        onehot, weighted, (((1,), (1,)), ((0,), (0,))), preferred_element_type=F32
-    ).astype(BF16)
-    normed_grad = lax.psum_scatter(spread, "exp", scatter_dimension=0, tiled=False).astype(F32)
+    returned = lax.all_to_all(weighted, "exp", split_axis=0, concat_axis=0, tiled=True)
+    normed_grad = dot(sent, returned.reshape(experts * capacity, width), 0, 0)
 
     scaled = normed_grad * norm_gain[None, :]
     dy = (

time: 334 us -> 337 us (level)
  starting transfers between devices: 1.54 us -> 18.4 us
  blocking collectives: 10.1 us -> 0 us
  waiting for transfers between devices: 234 us -> 229 us
  matrix products: 48.6 us -> 53.5 us
    all_to_all x0 -> x3, waiting for transfers between devices: none -> 221 us  [the longest x1 133 us: local(): lax.all_to_all(send_grads, 'exp', split_axis=0, concat_axis=0, tiled=True)]
    reduce_scatter x1 -> x0, waiting for transfers between devices: 96.3 us -> none  [local(): lax.psum_scatter(spread, 'exp', scatter_dimension=0, tiled=False)]
    all_gather x1 -> x0, waiting for transfers between devices: 63.9 us -> none  [local(): all_grads = lax.all_gather(grads, 'exp')]
    all_gather x1, waiting for transfers between devices: 61.9 us -> 0.01 us  [local(): all_normed = lax.all_gather(normed, 'exp')]
    all_to_all x0 -> x3, starting transfers between devices: none -> 17.1 us  [the longest x1 6.24 us: local(): lax.all_to_all(table, 'exp', split_axis=0, concat_axis=0, tiled=True)]
    dot_general x8 -> x11, matrix products: 33.3 us -> 48.6 us  [dot(): lax.dot_general(a, b, (((ca,), (cb,)), ((), ())), preferred_element_type=...]
    dot_general x3 -> x1, matrix products: 15.2 us -> 4.77 us  [local(): lax.dot_general(held.astype(BF16), all_normed, (((2,), (1,)), ((0,), (0,)...]
    all_to_all x1 -> x0, blocking collectives: 10.1 us -> none  [local(): lax.all_to_all(table, 'exp', split_axis=0, concat_axis=0, tiled=True)]
  transfers between devices with their start and end apart: 4 -> 5, of which waited for: 4 -> 3; matrix products, arithmetic and copies ran while one was open for 6% -> 7% of each run, Pallas kernels for 0% -> 0%
where the time goes in v3:
time: 337 us; the launch traced here: 336 us
  waiting for transfers between devices  229 us (68%)
  matrix products  53.5 us (16%)
  starting transfers between devices  18.4 us (5%)
  between operations  14.2 us (4%)
  local copies, waits for them, and re-layouts  13.5 us (4%)
  other arithmetic  6.16 us (2%)
    all_to_all x1, waiting for transfers between devices, local(): lax.all_to_all(send_grads, 'exp', split_axis=0, concat_axis=0, tiled=True)  133 us
    all_to_all x1, waiting for transfers between devices, local(): lax.all_to_all(weighted, 'exp', split_axis=0, concat_axis=0, tiled=True)  87.6 us
    dot_general x11, matrix products, dot(): lax.dot_general(a, b, (((ca,), (cb,)), ((), ())), preferred_element_type=...  48.6 us
    ppermute x1, waiting for transfers between devices, incoming_state(): return lax.ppermute(state.astype(BF16), 'seq', [(1, 0)])  7.96 us
  transfers between devices with their start and end apart: 5, of which 3 were waited for; matrix products, arithmetic and copies ran while one was open for 7% of the time, Pallas kernels for 0%

profile of v3, /device:TPU:10, one launch (start us, length us, event | category | flops | bytes accessed | tf_op | source)
XLA Modules:
  0.0 336.1 jit_solution(3785815838491579680)
XLA Ops:
  7.2 0.0 copy-start
  7.2 0.0 all-gather.2.cloned.1.call-start
  7.2 1.4 fusion.21
  8.6 2.0 fusion.23
  10.7 0.0 all-gather.2.cloned.1.call-update
  10.7 0.7 copy.55
  11.4 0.7 copy.56
  12.1 0.6 select_reduce_fusion.1
  12.7 6.2 %all-to-all-start = ((f32[16,1,128]{2,1,0:T(1,128)}), f32[16,1,128]{2,1,0:T(1,128)S(1)}, u32[]{:S(2)}, u32[]{:S(2)}) async-start(f32[16,1,128]{2,1,0:T(1,128)} %bitcast.2), calls=%async_computation | async-start | bytes 16384 | tf_op jit(solution)/shard_map/all_to_all | solution.py:105
  18.9 0.7 broadcast_compare_fusion
  19.6 0.1 convolution_convert_fusion.4
  19.8 0.1 fusion.27
  19.9 4.2 %convolution_convert_fusion.1 = bf16[1024,2048]{1,0:T(8,128)(2,1)} fusion(pred[1024,128]{1,0:T(32,128)(4,1)S(1)} %bitcast.109, bf16[1,128,2048]{2,1,0:T(8,128)(2,1)} %param.13), kind=kOutput, calls=%fused_computation.2 | convolution fusion | flops 538968064 | bytes 4849664 | tf_op jit(solution)/shard_map/dot_general | solution.py:17
  24.1 0.0 all-to-all-done
  24.1 6.0 %all-to-all-start.1 = ((bf16[16,64,2048]{2,1,0:T(8,128)(2,1)}), bf16[16,64,2048]{2,1,0:T(8,128)(2,1)}, u32[]{:S(2)}, u32[]{:S(2)}) async-start(bf16[16,64,2048]{2,1,0:T(8,128)(2,1)} %bitcast.103), calls=%async_computation.1 | async-start | bytes 8388608 | tf_op jit(solution)/shard_map/all_to_all | solution.py:118
  30.2 0.1 convolution_convert_fusion.3
  30.3 0.2 select_reduce_fusion
  30.5 0.1 mul.68
  30.6 133.1 %all-to-all-done.1 = bf16[16,64,2048]{2,1,0:T(8,128)(2,1)} async-done(((bf16[16,64,2048]{2,1,0:T(8,128)(2,1)}), bf16[16,64,2048]{2,1,0:T(8,128)(2,1)}, u32[]{:S(2)}, u32[]{:S(2)}) %all-to-all-start.1) | async-done | bytes 4194336 | tf_op jit(solution)/shard_map/all_to_all | solution.py:118
  163.7 7.8 %fusion.7 = f32[1024,704]{0,1:T(8,128)} fusion(bf16[1024,2048]{1,0:T(8,128)(2,1)} %bitcast.8, bf16[1,704,2048]{2,1,0:T(8,128)(2,1)} %param.19), kind=kOutput, calls=%fused_computation.10 | convolution fusion | flops 2952790016 | bytes 9961472 | tf_op jit(solution)/shard_map/dot_general | solution.py:17
  171.6 4.8 %convolution_convert_fusion = bf16[16,64,2048]{2,1,0:T(8,128)(2,1)S(1)} fusion(bf16[16,128,2048]{2,1,0:T(8,128)(2,1)} %all-gather.2.cloned.1.call-done, s32[16,128]{1,0:T(8,128)S(1)} %convolution_convert_fusion.3, pred[16,128]{1,0:T(8,128)(4,1)S(1)} %compare_bitcast_fusion), kind=kOutput, calls=%fused_computation.1 | convolution fusion | flops 539230208 | bytes 12593152 | tf_op jit(solution)/shard_map/dot_general | solution.py:124
  176.4 1.9 copy-done.5
  178.3 0.0 copy-done.12
  178.3 4.8 %fusion.2 = f32[1024,704]{0,1:T(8,128)} fusion(bf16[1024,2048]{1,0:T(8,128)(2,1)S(1)} %bitcast.104, bf16[1,2048,704]{1,2,0:T(8,128)(2,1)S(1)} %copy-done.12), kind=kOutput, calls=%fused_computation.5 | convolution fusion | flops 2952790016 | bytes 9961472 | tf_op jit(solution)/shard_map/dot_general | solution.py:17
  183.1 13.6 %fusion = f32[1024,2048]{1,0:T(8,128)} fusion(bf16[1,2048,704]{1,2,0:T(8,128)(2,1)} %param.17, f32[1024,704]{0,1:T(8,128)} %fusion.2, f32[1024,704]{0,1:T(8,128)} %fusion.7, bf16[1024,2048]{1,0:T(8,128)(2,1)} %bitcast.105, bf16[1,2048,704]{1,2,0:T(8,128)(2,1)S(1)} %copy-done), kind=kOutput, calls=%fused_computation.3 | convolution fusion | flops 5912788992 | bytes 24117248 | tf_op jit(solution)/shard_map/dot_general | solution.py:17
  196.7 9.1 %multiply_convert_fusion = bf16[1024,2048]{1,0:T(8,128)(2,1)} fusion(f32[1024,2048]{1,0:T(8,128)} %fusion, f32[1024]{0:T(1024)S(1)} %mul.68, bf16[1,2048,704]{1,2,0:T(8,128)(2,1)S(1)} %copy-done, f32[1024,704]{0,1:T(8,128)} %fusion.7, f32[1024,704]{0,1:T(8,128)} %fusion.2), kind=kOutput, calls=%fused_computation | convolution fusion | flops 2963406848 | bytes 21237760 | tf_op jit(solution)/shard_map/dot_general | solution.py:17
  205.8 4.8 %all-to-all-start.2 = ((bf16[16,64,2048]{2,1,0:T(8,128)(2,1)}), bf16[16,64,2048]{2,1,0:T(8,128)(2,1)}, u32[]{:S(2)}, u32[]{:S(2)}) async-start(bf16[16,64,2048]{2,1,0:T(8,128)(2,1)} %bitcast.106), calls=%async_computation.2 | async-start | bytes 8388608 | tf_op jit(solution)/shard_map/all_to_all | solution.py:139
  210.6 0.0 copy-start.7
  210.6 0.0 copy-start.11
  210.6 0.2 fusion.32
  210.8 0.2 slice_reduce_fusion
  211.0 0.7 fusion.59
  211.7 1.1 broadcast_in_dim.77
  212.8 2.5 copy.46
  215.3 87.6 %all-to-all-done.2 = bf16[16,64,2048]{2,1,0:T(8,128)(2,1)} async-done(((bf16[16,64,2048]{2,1,0:T(8,128)(2,1)}), bf16[16,64,2048]{2,1,0:T(8,128)(2,1)}, u32[]{:S(2)}, u32[]{:S(2)}) %all-to-all-start.2) | async-done | bytes 4194336 | tf_op jit(solution)/shard_map/all_to_all | solution.py:139
  302.9 3.2 multiply_reduce_fusion
  306.1 0.3 add_convert_fusion.dy_ref
  306.5 0.8 copy-done.9
  307.3 1.2 fusion.13
  308.5 1.3 collective-permute-start
  309.8 0.1 copy.45.cum_ref
  309.9 1.8 broadcast_in_dim.76
  311.7 2.6 copy.48
  314.2 1.0 copy-done.2
  315.3 1.6 shard_map.139
  316.9 8.0 %collective-permute-done = bf16[128,2048]{0,1:T(8,128)(2,1)} collective-permute-done((bf16[128,2048]{0,1:T(8,128)(2,1)}, bf16[128,2048]{0,1:T(8,128)(2,1)}, u32[]{:S(2)}, u32[]{:S(2)}) %collective-permute-start) | collective-permute-done | bytes 524320 | tf_op jit(solution)/shard_map/ppermute | solution.py:62
  324.8 2.3 fusion.20
  327.1 2.1 fusion.14
  (25 shorter events, 0.1 us)
Async XLA Ops:
  7.2 175.9 %copy-start = (bf16[1,2048,704]{1,2,0:T(8,128)(2,1)S(1)}, bf16[1,2048,704]{1,2,0:T(8,128)(2,1)}, u32[]{:S(2)}) copy-start(bf16[1,2048,704]{1,2,0:T(8,128)(2,1)} %param.18) | copy-start | bytes 8650756
  7.2 164.4 %all-gather.2.cloned.1.call-start = ((), (), s32[]{:S(2)}) async-start(), calls=%async_computation.3 | async-start | bytes 8912896 | tf_op jit(solution)/shard_map/all_gather | solution.py:106
  12.7 11.5 %all-to-all-start = ((f32[16,1,128]{2,1,0:T(1,128)}), f32[16,1,128]{2,1,0:T(1,128)S(1)}, u32[]{:S(2)}, u32[]{:S(2)}) async-start(f32[16,1,128]{2,1,0:T(1,128)} %bitcast.2), calls=%async_computation | async-start | bytes 16384 | tf_op jit(solution)/shard_map/all_to_all | solution.py:105
  24.1 139.6 %all-to-all-start.1 = ((bf16[16,64,2048]{2,1,0:T(8,128)(2,1)}), bf16[16,64,2048]{2,1,0:T(8,128)(2,1)}, u32[]{:S(2)}, u32[]{:S(2)}) async-start(bf16[16,64,2048]{2,1,0:T(8,128)(2,1)} %bitcast.103), calls=%async_computation.1 | async-start | bytes 8388608 | tf_op jit(solution)/shard_map/all_to_all | solution.py:118
  171.6 6.7 %copy-start.12 = (bf16[1,2048,704]{1,2,0:T(8,128)(2,1)S(1)}, bf16[1,2048,704]{1,2,0:T(8,128)(2,1)}, u32[]{:S(2)}) copy-start(bf16[1,2048,704]{1,2,0:T(8,128)(2,1)} %param.17) | copy-start | bytes 8650756
  176.4 2.0 copy-start.5
  205.8 4.8 %copy-start.13 = (f32[1,128,32]{1,2,0:T(8,128)S(1)}, f32[1,128,32]{1,2,0:T(8,128)}, u32[]{:S(2)}) copy-start(f32[1,128,32]{1,2,0:T(8,128)} %param.23) | copy-start | bytes 49156
  205.8 97.1 %all-to-all-start.2 = ((bf16[16,64,2048]{2,1,0:T(8,128)(2,1)}), bf16[16,64,2048]{2,1,0:T(8,128)(2,1)}, u32[]{:S(2)}, u32[]{:S(2)}) async-start(bf16[16,64,2048]{2,1,0:T(8,128)(2,1)} %bitcast.106), calls=%async_computation.2 | async-start | bytes 8388608 | tf_op jit(solution)/shard_map/all_to_all | solution.py:139
  210.6 92.3 %copy-start.7 = (bf16[1,128,2048]{2,1,0:T(8,128)(2,1)S(1)}, bf16[1,128,2048]{2,1,0:T(8,128)(2,1)}, u32[]{:S(2)}) copy-start(bf16[1,128,2048]{2,1,0:T(8,128)(2,1)} %param.12) | copy-start | bytes 1572868
  210.6 92.3 %copy-start.11 = (f32[2048]{0:T(1024)S(1)}, f32[2048]{0:T(1024)}, u32[]{:S(2)}) copy-start(f32[2048]{0:T(1024)} %param.14) | copy-start | bytes 24580
  215.3 91.2 %copy-start.3 = (bf16[1,128,128]{2,1,0:T(8,128)(2,1)S(1)}, bf16[1,128,128]{2,1,0:T(8,128)(2,1)}, u32[]{:S(2)}) copy-start(bf16[1,128,128]{2,1,0:T(8,128)(2,1)} %param.22) | copy-start | bytes 98308
  302.9 3.2 copy-start.8
  302.9 3.2 copy-start.10
  306.1 1.2 copy-start.9
  307.3 9.5 %copy-start.1 = (bf16[128,2048]{1,0:T(8,128)(2,1)}, bf16[128,2048]{1,0:T(8,128)(2,1)S(1)}, u32[]{:S(2)}) copy-start(bf16[128,2048]{1,0:T(8,128)(2,1)S(1)} %add_convert_fusion.dy_ref) | copy-start | bytes 1572868
  307.3 6.9 %copy-start.4 = (bf16[1,128,128]{2,1,0:T(8,128)(2,1)S(1)}, bf16[1,128,128]{2,1,0:T(8,128)(2,1)}, u32[]{:S(2)}) copy-start(bf16[1,128,128]{2,1,0:T(8,128)(2,1)} %param.21) | copy-start | bytes 98308
  308.5 16.3 %collective-permute-start = (bf16[128,2048]{0,1:T(8,128)(2,1)}, bf16[128,2048]{0,1:T(8,128)(2,1)}, u32[]{:S(2)}, u32[]{:S(2)}) collective-permute-start(bf16[128,2048]{0,1:T(8,128)(2,1)} %fusion.13), channel_id=1, source_target_pairs={{16,0},{17,1},{18,2},{19,3},{20,4},{21,5},{22,6},{23,7},{24,8},{25... | collective-permute-start | bytes 1572872 | tf_op jit(solution)/shard_map/ppermute | solution.py:62
  314.2 1.0 copy-start.2
  315.3 11.8 %copy-start.6 = (f32[128,2048]{1,0:T(8,128)S(1)}, f32[128,2048]{1,0:T(8,128)}, u32[]{:S(2)}) copy-start(f32[128,2048]{1,0:T(8,128)} %copy.48) | copy-start | bytes 3145732
Sparse Core Ops, SparseCore 0:
  10.8 132.7 all-gather.1

commit v4 on v3

--- a/solution.py
+++ b/solution.py
@@ -72,6 +72,28 @@
     return carried.astype(BF16)
 
 
+def gather_beside(rows):
+    count = lax.axis_size("exp")
+    if count != 16:
+        return lax.all_gather(rows, "exp")
+    depth = count // 4
+    me = lax.axis_index("exp")
+    z, x, core = me // 4, (me // 2) % 2, me % 2
+    out = jnp.zeros((depth, 2, 2) + rows.shape, rows.dtype)
+    for step in range(depth):
+        block = rows
+        if step:
+            block = lax.ppermute(rows, "exp", [(i, (i + 4 * step) % count) for i in range(count)])
+        other = lax.ppermute(block, "exp", [(i, i ^ 2) for i in range(count)])
+        pair = jnp.where(x == 0, jnp.stack([block, other]), jnp.stack([other, block]))
+        swapped = lax.ppermute(pair, "exp", [(i, i ^ 1) for i in range(count)])
+        quad = jnp.where(
+            core == 0, jnp.stack([pair, swapped], 1), jnp.stack([swapped, pair], 1)
+        )
+        out = lax.dynamic_update_index_in_dim(out, quad, (z - step + depth) % depth, 0)
+    return out.reshape((count,) + rows.shape)
+
+
 def local(
     stream_input,
     grad_output,
@@ -114,19 +136,20 @@
         return (slots[:, None, :] == places) & chosen[:, None, :]
 
     sent = picks(table).astype(BF16).reshape(experts * capacity, tokens)
-    send_grads = dot(sent, grads, 1, 0).astype(BF16).reshape(experts, capacity, width)
-    grad_rows = lax.all_to_all(send_grads, "exp", split_axis=0, concat_axis=0, tiled=True)
-    grad_rows = grad_rows.reshape(experts * capacity, width)
+    all_grads = gather_beside(grads)
 
     held = picks(own_gates)
     slot_gates = jnp.sum(jnp.where(held, own_gates[:, None, :], 0.0), axis=2).reshape(-1, 1)
-    normed_rows = (
-        lax.dot_general(
-            held.astype(BF16), all_normed, (((2,), (1,)), ((0,), (0,))), preferred_element_type=F32
+    onehot = held.astype(BF16)
+
+    def take(rows):
+        taken = lax.dot_general(
+            onehot, rows, (((2,), (1,)), ((0,), (0,))), preferred_element_type=F32
         )
-        .astype(BF16)
-        .reshape(experts * capacity, width)
-    )
+        return taken.astype(BF16).reshape(experts * capacity, width)
+
+    normed_rows = take(all_normed)
+    grad_rows = take(all_grads)
     gate_weight, up_weight, down_weight = w_gate[0], w_up[0], w_down[0]
     back = dot(grad_rows, down_weight, 1, 1)
     gate_pre = dot(normed_rows, gate_weight, 1, 0)

time: 337 us -> 327 us (0.970)
  waiting for transfers between devices: 229 us -> 179 us
  other arithmetic: 6.16 us -> 27.8 us
  local copies, waits for them, and re-layouts: 13.5 us -> 26.2 us
  starting transfers between devices: 18.4 us -> 26.6 us
    all_to_all x1 -> x0, waiting for transfers between devices: 133 us -> none  [local(): lax.all_to_all(send_grads, 'exp', split_axis=0, concat_axis=0, tiled=True)]
    ppermute x0 -> x11, waiting for transfers between devices: none -> 68.1 us  [the longest x4 37.6 us: gather_beside(): other = lax.ppermute(block, 'exp', [(i, i ^ 2) for i in range(count)])]
    all_to_all x1, waiting for transfers between devices: 0.01 us -> 15.8 us  [local(): lax.all_to_all(table, 'exp', split_axis=0, concat_axis=0, tiled=True)]
    ppermute x0 -> x11, starting transfers between devices: none -> 12.5 us  [the longest x4 7.59 us: gather_beside(): other = lax.ppermute(block, 'exp', [(i, i ^ 2) for i in range(count)])]
    dynamic_update_slice x0 -> x4, other arithmetic: none -> 9.12 us  [gather_beside(): lax.dynamic_update_index_in_dim(out, quad, (z - step + depth) % depth, 0)]
    dynamic_update_slice x0 -> x1, local copies, waits for them, and re-layouts: none -> 8.26 us  [gather_beside(): lax.dynamic_update_index_in_dim(out, quad, (z - step + depth) % depth, 0)]
    select_n x0 -> x4, other arithmetic: none -> 7.49 us  [gather_beside(): jnp.where(x == 0, jnp.stack([block, other]), jnp.stack([other, block]))]
    dot_general x11 -> x10, matrix products: 48.6 us -> 41.4 us  [dot(): lax.dot_general(a, b, (((ca,), (cb,)), ((), ())), preferred_element_type=...]
  transfers between devices with their start and end apart: 5 -> 15, of which waited for: 3 -> 6; matrix products, arithmetic and copies ran while one was open for 7% -> 17% of each run, Pallas kernels for 0% -> 0%
where the time goes in v4:
time: 327 us; the launch traced here: 326 us
  waiting for transfers between devices  179 us (55%)
  matrix products  51.2 us (16%)
  other arithmetic  27.8 us (9%)
  starting transfers between devices  26.6 us (8%)
  local copies, waits for them, and re-layouts  26.2 us (8%)
  between operations  14.3 us (4%)
    all_to_all x1, waiting for transfers between devices, local(): lax.all_to_all(weighted, 'exp', split_axis=0, concat_axis=0, tiled=True)  86.7 us
    dot_general x10, matrix products, dot(): lax.dot_general(a, b, (((ca,), (cb,)), ((), ())), preferred_element_type=...  41.4 us
    ppermute x4, waiting for transfers between devices, gather_beside(): other = lax.ppermute(block, 'exp', [(i, i ^ 2) for i in range(count)])  37.6 us
    ppermute x3, waiting for transfers between devices, gather_beside(): lax.ppermute(rows, 'exp', [(i, (i + 4 * step) % count) for i in range(cou...  30.5 us
    all_to_all x1, waiting for transfers between devices, local(): lax.all_to_all(table, 'exp', split_axis=0, concat_axis=0, tiled=True)  15.8 us
    dot_general x2, matrix products, take(): lax.dot_general(onehot, rows, (((2,), (1,)), ((0,), (0,))), preferred_ele...  9.54 us
    dynamic_update_slice x4, other arithmetic, gather_beside(): lax.dynamic_update_index_in_dim(out, quad, (z - step + depth) % depth, 0)  9.12 us
    dynamic_update_slice x1, local copies, waits for them, and re-layouts, gather_beside(): lax.dynamic_update_index_in_dim(out, quad, (z - step + depth) % depth, 0)  8.26 us
  transfers between devices with their start and end apart: 15, of which 6 were waited for; matrix products, arithmetic and copies ran while one was open for 17% of the time, Pallas kernels for 0%

profile of v4, /device:TPU:10, one launch (start us, length us, event | category | flops | bytes accessed | tf_op | source)
XLA Modules:
  0.0 326.2 jit_solution(1615708870790920054)
XLA Ops:
  7.2 1.4 fusion.24
  8.7 2.0 fusion.26
  10.7 1.6 collective-permute-start.2
  14.3 5.2 %all-to-all-start = ((f32[16,1,128]{2,1,0:T(1,128)}), f32[16,1,128]{2,1,0:T(1,128)S(1)}, u32[]{:S(2)}, u32[]{:S(2)}) async-start(f32[16,1,128]{2,1,0:T(1,128)} %bitcast.2), calls=%async_computation | async-start | bytes 16384 | tf_op jit(solution)/shard_map/all_to_all | solution.py:127
  20.1 2.4 collective-permute-start.5
  23.1 15.8 %all-to-all-done = f32[16,1,128]{2,1,0:T(1,128)S(1)} async-done(((f32[16,1,128]{2,1,0:T(1,128)}), f32[16,1,128]{2,1,0:T(1,128)S(1)}, u32[]{:S(2)}, u32[]{:S(2)}) %all-to-all-start) | async-done | bytes 8224 | tf_op jit(solution)/shard_map/all_to_all | solution.py:127
  39.0 4.9 %collective-permute-start.3 = (bf16[128,2048]{1,0:T(8,128)(2,1)}, bf16[128,2048]{1,0:T(8,128)(2,1)}, u32[]{:S(2)}, u32[]{:S(2)}) collective-permute-start(bf16[128,2048]{1,0:T(8,128)(2,1)} %collective-permute-done.2), channel_id=1, source_target_pairs={{0,2},{1,3},{2,0},{3,1},{4,6},{5,7},{6,4},{7,5},{8,10},{9,11},{10,... | collective-permute-start | bytes 1572872 | tf_op jit(solution)/shard_map/ppermute | solution.py:87
  44.2 30.5 %collective-permute-done.5 = bf16[128,2048]{1,0:T(8,128)(2,1)} collective-permute-done((bf16[128,2048]{1,0:T(8,128)(2,1)}, bf16[128,2048]{1,0:T(8,128)(2,1)}, u32[]{:S(2)}, u32[]{:S(2)}) %collective-permute-start.5) | collective-permute-done | bytes 524320 | tf_op jit(solution)/shard_map/ppermute | solution.py:86
  75.2 1.9 maximum_select_fusion.4
  77.2 1.6 collective-permute-start.9
  78.8 1.4 fusion.27
  80.2 1.8 maximum_select_fusion.6
  82.2 18.3 %collective-permute-done.6 = bf16[128,2048]{1,0:T(8,128)(2,1)S(1)} collective-permute-done((bf16[128,2048]{1,0:T(8,128)(2,1)}, bf16[128,2048]{1,0:T(8,128)(2,1)S(1)}, u32[]{:S(2)}, u32[]{:S(2)}) %collective-permute-start.6) | collective-permute-done | bytes 524320 | tf_op jit(solution)/shard_map/ppermute | solution.py:87
  100.6 1.4 maximum_select_fusion.7
  102.0 19.3 %collective-permute-done.9 = bf16[128,2048]{1,0:T(8,128)(2,1)S(1)} collective-permute-done((bf16[128,2048]{1,0:T(8,128)(2,1)}, bf16[128,2048]{1,0:T(8,128)(2,1)S(1)}, u32[]{:S(2)}, u32[]{:S(2)}) %collective-permute-start.9) | collective-permute-done | bytes 524320 | tf_op jit(solution)/shard_map/ppermute | solution.py:87
  121.3 2.4 maximum_select_fusion.9
  123.7 1.9 fusion.30
  125.7 1.8 fusion.28
  127.5 4.3 %broadcast_in_dim.81 = bf16[4,2,2,128,2048]{4,3,1,2,0:T(8,128)(2,1)} broadcast(bf16[]{:T(256)} %constant.89.clone.1), dimensions={} | broadcast | bytes 8388610 | tf_op jit(solution)/shard_map/broadcast_in_dim | solution.py:82
  131.8 1.8 fusion.15
  133.6 1.8 fusion.16
  135.4 1.8 fusion.17
  137.3 8.3 %copy.68 = bf16[4,2,2,128,2048]{4,3,2,1,0:T(8,128)(2,1)} copy(bf16[4,2,2,128,2048]{4,3,1,2,0:T(8,128)(2,1)} %fusion.17) | data formatting | bytes 16777216 | tf_op jit(solution)/shard_map/jit(dynamic_update_index_in_dim)/dynamic_update_slice | solution.py:93
  145.5 3.7 %copy_dynamic-update-slice_fusion = bf16[4,2,2,128,2048]{4,3,2,1,0:T(8,128)(2,1)} fusion(bf16[4,2,2,128,2048]{4,3,2,1,0:T(8,128)(2,1)} %copy.68, s32[]{:T(128)S(6)} %select_n.236, bf16[1,2,1,128,2048]{4,3,1,2,0:T(8,128)(2,1)} %bitcast.31, bf16[1,2,1,128,2048]{4,3,1,2,0:T(8,128)(2,1)S(1)} %get-tuple-element.12, pred[]{:T(512)S(6)} %eq.70), kind=kLoop, calls=%fused_computation.31 | loop fusion | flops 3145728 | bytes 4194309 | tf_op jit(solution)/shard_map/jit(dynamic_update_index_in_dim)/dynamic_update_slice | solution.py:93
  149.2 4.8 %convolution_convert_fusion.1 = bf16[16,64,2048]{2,1,0:T(8,128)(2,1)S(1)} fusion(bf16[16,128,2048]{2,1,0:T(8,128)(2,1)} %bitcast.141, s32[16,128]{1,0:T(8,128)S(1)} %convolution_convert_fusion.3, pred[16,128]{1,0:T(8,128)(4,1)S(1)} %compare_bitcast_fusion), kind=kOutput, calls=%fused_computation.2 | convolution fusion | flops 539230208 | bytes 12593152 | tf_op jit(solution)/shard_map/dot_general | solution.py:146
  154.0 4.7 %fusion.7 = f32[1024,704]{0,1:T(8,128)} fusion(bf16[1024,2048]{1,0:T(8,128)(2,1)S(1)} %bitcast.144, bf16[1,704,2048]{2,1,0:T(8,128)(2,1)S(1)} %copy-done.13), kind=kOutput, calls=%fused_computation.10 | convolution fusion | flops 2952790016 | bytes 9961472 | tf_op jit(solution)/shard_map/dot_general | solution.py:17
  158.7 4.8 %convolution_convert_fusion = bf16[16,64,2048]{2,1,0:T(8,128)(2,1)S(1)} fusion(bf16[16,128,2048]{2,1,0:T(8,128)(2,1)} %all-gather.2.cloned.1.call-done, s32[16,128]{1,0:T(8,128)S(1)} %convolution_convert_fusion.3, pred[16,128]{1,0:T(8,128)(4,1)S(1)} %compare_bitcast_fusion), kind=kOutput, calls=%fused_computation.1 | convolution fusion | flops 539230208 | bytes 12593152 | tf_op jit(solution)/shard_map/dot_general | solution.py:146
  163.5 2.0 copy-done.5
  165.5 4.9 %fusion.2 = f32[1024,704]{0,1:T(8,128)} fusion(bf16[1024,2048]{1,0:T(8,128)(2,1)S(1)} %bitcast.142, bf16[1,2048,704]{1,2,0:T(8,128)(2,1)S(1)} %copy-done.14), kind=kOutput, calls=%fused_computation.5 | convolution fusion | flops 2952790016 | bytes 9961472 | tf_op jit(solution)/shard_map/dot_general | solution.py:17
  170.4 13.6 %fusion = f32[1024,2048]{1,0:T(8,128)} fusion(bf16[1,2048,704]{1,2,0:T(8,128)(2,1)} %param.17, f32[1024,704]{0,1:T(8,128)} %fusion.2, f32[1024,704]{0,1:T(8,128)} %fusion.7, bf16[1024,2048]{1,0:T(8,128)(2,1)} %bitcast.143, bf16[1,2048,704]{1,2,0:T(8,128)(2,1)S(1)} %copy-done), kind=kOutput, calls=%fused_computation.3 | convolution fusion | flops 5912788992 | bytes 24117248 | tf_op jit(solution)/shard_map/dot_general | solution.py:17
  184.1 9.1 %multiply_convert_fusion = bf16[1024,2048]{1,0:T(8,128)(2,1)} fusion(f32[1024,2048]{1,0:T(8,128)} %fusion, f32[1024]{0:T(1024)S(1)} %mul.68, bf16[1,2048,704]{1,2,0:T(8,128)(2,1)S(1)} %copy-done, f32[1024,704]{0,1:T(8,128)} %fusion.7, f32[1024,704]{0,1:T(8,128)} %fusion.2), kind=kOutput, calls=%fused_computation | convolution fusion | flops 2963406848 | bytes 21237760 | tf_op jit(solution)/shard_map/dot_general | solution.py:17
  193.2 7.5 %all-to-all-start.1 = ((bf16[16,64,2048]{2,1,0:T(8,128)(2,1)}), bf16[16,64,2048]{2,1,0:T(8,128)(2,1)}, u32[]{:S(2)}, u32[]{:S(2)}) async-start(bf16[16,64,2048]{2,1,0:T(8,128)(2,1)} %bitcast.150), calls=%async_computation.1 | async-start | bytes 8388608 | tf_op jit(solution)/shard_map/all_to_all | solution.py:162
  201.1 0.7 fusion.71
  201.8 1.1 broadcast_in_dim.86
  202.9 2.6 copy.71
  205.4 0.7 broadcast_compare_fusion
  206.3 86.7 %all-to-all-done.1 = bf16[16,64,2048]{2,1,0:T(8,128)(2,1)} async-done(((bf16[16,64,2048]{2,1,0:T(8,128)(2,1)}), bf16[16,64,2048]{2,1,0:T(8,128)(2,1)}, u32[]{:S(2)}, u32[]{:S(2)}) %all-to-all-start.1) | async-done | bytes 4194336 | tf_op jit(solution)/shard_map/all_to_all | solution.py:162
  293.0 3.2 multiply_reduce_fusion
  296.6 0.8 copy-done.11
  297.4 1.2 fusion.13
  298.6 1.3 collective-permute-start.11
  300.0 1.8 broadcast_in_dim.85
  301.7 2.5 copy.73
  304.3 1.0 copy-done.2
  305.3 1.6 shard_map.139
  306.9 8.0 %collective-permute-done.11 = bf16[128,2048]{0,1:T(8,128)(2,1)} collective-permute-done((bf16[128,2048]{0,1:T(8,128)(2,1)}, bf16[128,2048]{0,1:T(8,128)(2,1)}, u32[]{:S(2)}, u32[]{:S(2)}) %collective-permute-start.11) | collective-permute-done | bytes 524320 | tf_op jit(solution)/shard_map/ppermute | solution.py:62
  314.9 2.3 fusion.23
  317.2 2.1 fusion.14
  (61 shorter events, 5.6 us)
Async XLA Ops:
  7.2 163.3 %copy-start = (bf16[1,2048,704]{1,2,0:T(8,128)(2,1)S(1)}, bf16[1,2048,704]{1,2,0:T(8,128)(2,1)}, u32[]{:S(2)}) copy-start(bf16[1,2048,704]{1,2,0:T(8,128)(2,1)} %param.18) | copy-start | bytes 8650756
  7.2 71.6 %copy-start.7 = (bf16[1,128,2048]{2,1,0:T(8,128)(2,1)S(1)}, bf16[1,128,2048]{2,1,0:T(8,128)(2,1)}, u32[]{:S(2)}) copy-start(bf16[1,128,2048]{2,1,0:T(8,128)(2,1)} %param.13) | copy-start | bytes 1572868
  7.2 151.5 %all-gather.2.cloned.1.call-start = ((), (), s32[]{:S(2)}) async-start(), calls=%async_computation.2 | async-start | bytes 8912896 | tf_op jit(solution)/shard_map/all_gather | solution.py:128
  10.7 28.3 %collective-permute-start.2 = (bf16[128,2048]{1,0:T(8,128)(2,1)}, bf16[128,2048]{1,0:T(8,128)(2,1)}, u32[]{:S(2)}, u32[]{:S(2)}) collective-permute-start(bf16[128,2048]{1,0:T(8,128)(2,1)} %bitcast.145), channel_id=1, source_target_pairs={{0,4},{1,5},{2,6},{3,7},{4,8},{5,9},{6,10},{7,11},{8,12},{9,13},{1... | collective-permute-start | bytes 1572872 | tf_op jit(solution)/shard_map/ppermute | solution.py:86
  14.3 24.5 %all-to-all-start = ((f32[16,1,128]{2,1,0:T(1,128)}), f32[16,1,128]{2,1,0:T(1,128)S(1)}, u32[]{:S(2)}, u32[]{:S(2)}) async-start(f32[16,1,128]{2,1,0:T(1,128)} %bitcast.2), calls=%async_computation | async-start | bytes 16384 | tf_op jit(solution)/shard_map/all_to_all | solution.py:127
  19.6 55.6 %collective-permute-start = (bf16[128,2048]{1,0:T(8,128)(2,1)}, bf16[128,2048]{1,0:T(8,128)(2,1)}, u32[]{:S(2)}, u32[]{:S(2)}) collective-permute-start(bf16[128,2048]{1,0:T(8,128)(2,1)} %bitcast.146), channel_id=1, source_target_pairs={{0,2},{1,3},{2,0},{3,1},{4,6},{5,7},{6,4},{7,5},{8,10},{9,11},{10,... | collective-permute-start | bytes 1572872 | tf_op jit(solution)/shard_map/ppermute | solution.py:87
  20.1 54.5 %collective-permute-start.5 = (bf16[128,2048]{1,0:T(8,128)(2,1)}, bf16[128,2048]{1,0:T(8,128)(2,1)}, u32[]{:S(2)}, u32[]{:S(2)}) collective-permute-start(bf16[128,2048]{1,0:T(8,128)(2,1)} %bitcast.147), channel_id=1, source_target_pairs={{0,8},{1,9},{2,10},{3,11},{4,12},{5,13},{6,14},{7,15},{8,0},{9,1},... | collective-permute-start | bytes 1572872 | tf_op jit(solution)/shard_map/ppermute | solution.py:86
  22.5 54.7 %collective-permute-start.8 = (bf16[128,2048]{1,0:T(8,128)(2,1)}, bf16[128,2048]{1,0:T(8,128)(2,1)}, u32[]{:S(2)}, u32[]{:S(2)}) collective-permute-start(bf16[128,2048]{1,0:T(8,128)(2,1)} %bitcast.148), channel_id=1, source_target_pairs={{0,12},{1,13},{2,14},{3,15},{4,0},{5,1},{6,2},{7,3},{8,4},{9,5},{1... | collective-permute-start | bytes 1572872 | tf_op jit(solution)/shard_map/ppermute | solution.py:86
  39.0 41.2 %collective-permute-start.3 = (bf16[128,2048]{1,0:T(8,128)(2,1)}, bf16[128,2048]{1,0:T(8,128)(2,1)}, u32[]{:S(2)}, u32[]{:S(2)}) collective-permute-start(bf16[128,2048]{1,0:T(8,128)(2,1)} %collective-permute-done.2), channel_id=1, source_target_pairs={{0,2},{1,3},{2,0},{3,1},{4,6},{5,7},{6,4},{7,5},{8,10},{9,11},{10,... | collective-permute-start | bytes 1572872 | tf_op jit(solution)/shard_map/ppermute | solution.py:87
  74.6 25.9 %collective-permute-start.6 = (bf16[128,2048]{1,0:T(8,128)(2,1)}, bf16[128,2048]{1,0:T(8,128)(2,1)S(1)}, u32[]{:S(2)}, u32[]{:S(2)}) collective-permute-start(bf16[128,2048]{1,0:T(8,128)(2,1)} %collective-permute-done.5), channel_id=1, source_target_pairs={{0,2},{1,3},{2,0},{3,1},{4,6},{5,7},{6,4},{7,5},{8,10},{9,11},{10,... | collective-permute-start | bytes 1572872 | tf_op jit(solution)/shard_map/ppermute | solution.py:87
  77.1 50.4 %collective-permute-start.1 = (bf16[2,128,2048]{2,1,0:T(8,128)(2,1)S(1)}, bf16[2,128,2048]{2,1,0:T(8,128)(2,1)S(1)}, u32[]{:S(2)}, u32[]{:S(2)}) collective-permute-start(bf16[2,128,2048]{2,1,0:T(8,128)(2,1)S(1)} %maximum_select_fusion.4), channel_id=1, source_target_pairs={{0,1},{1,0},{2,3},{3,2},{4,5},{5,4},{6,7},{7,6},{8,9},{9,8},{10,11... | collective-permute-start | bytes 3145736 | tf_op jit(solution)/shard_map/ppermute | solution.py:89
  77.2 44.2 %collective-permute-start.9 = (bf16[128,2048]{1,0:T(8,128)(2,1)}, bf16[128,2048]{1,0:T(8,128)(2,1)S(1)}, u32[]{:S(2)}, u32[]{:S(2)}) collective-permute-start(bf16[128,2048]{1,0:T(8,128)(2,1)} %collective-permute-done.8), channel_id=1, source_target_pairs={{0,2},{1,3},{2,0},{3,1},{4,6},{5,7},{6,4},{7,5},{8,10},{9,11},{10,... | collective-permute-start | bytes 1572872 | tf_op jit(solution)/shard_map/ppermute | solution.py:87
  82.0 51.6 %collective-permute-start.4 = (bf16[2,128,2048]{2,1,0:T(8,128)(2,1)S(1)}, bf16[2,128,2048]{2,1,0:T(8,128)(2,1)S(1)}, u32[]{:S(2)}, u32[]{:S(2)}) collective-permute-start(bf16[2,128,2048]{2,1,0:T(8,128)(2,1)S(1)} %maximum_select_fusion.6), channel_id=1, source_target_pairs={{0,1},{1,0},{2,3},{3,2},{4,5},{5,4},{6,7},{7,6},{8,9},{9,8},{10,11... | collective-permute-start | bytes 3145736 | tf_op jit(solution)/shard_map/ppermute | solution.py:89
  102.0 33.5 %collective-permute-start.7 = (bf16[2,128,2048]{2,1,0:T(8,128)(2,1)S(1)}, bf16[2,128,2048]{2,1,0:T(8,128)(2,1)S(1)}, u32[]{:S(2)}, u32[]{:S(2)}) collective-permute-start(bf16[2,128,2048]{2,1,0:T(8,128)(2,1)S(1)} %maximum_select_fusion.7), channel_id=1, source_target_pairs={{0,1},{1,0},{2,3},{3,2},{4,5},{5,4},{6,7},{7,6},{8,9},{9,8},{10,11... | collective-permute-start | bytes 3145736 | tf_op jit(solution)/shard_map/ppermute | solution.py:89
  123.7 21.8 %collective-permute-start.10 = (bf16[2,128,2048]{2,1,0:T(8,128)(2,1)}, bf16[2,128,2048]{2,1,0:T(8,128)(2,1)}, u32[]{:S(2)}, u32[]{:S(2)}) collective-permute-start(bf16[2,128,2048]{2,1,0:T(8,128)(2,1)} %maximum_select_fusion.9), channel_id=1, source_target_pairs={{0,1},{1,0},{2,3},{3,2},{4,5},{5,4},{6,7},{7,6},{8,9},{9,8},{10,11... | collective-permute-start | bytes 3145736 | tf_op jit(solution)/shard_map/ppermute | solution.py:89
  149.2 4.8 %copy-start.13 = (bf16[1,704,2048]{2,1,0:T(8,128)(2,1)S(1)}, bf16[1,704,2048]{2,1,0:T(8,128)(2,1)}, u32[]{:S(2)}) copy-start(bf16[1,704,2048]{2,1,0:T(8,128)(2,1)} %param.19) | copy-start | bytes 8650756
  158.7 6.8 %copy-start.14 = (bf16[1,2048,704]{1,2,0:T(8,128)(2,1)S(1)}, bf16[1,2048,704]{1,2,0:T(8,128)(2,1)}, u32[]{:S(2)}) copy-start(bf16[1,2048,704]{1,2,0:T(8,128)(2,1)} %param.17) | copy-start | bytes 8650756
  163.5 2.0 copy-start.5
  193.2 7.5 %copy-start.15 = (f32[1,128,32]{1,2,0:T(8,128)S(1)}, f32[1,128,32]{1,2,0:T(8,128)}, u32[]{:S(2)}) copy-start(f32[1,128,32]{1,2,0:T(8,128)} %param.23) | copy-start | bytes 49156
  193.2 99.8 %all-to-all-start.1 = ((bf16[16,64,2048]{2,1,0:T(8,128)(2,1)}), bf16[16,64,2048]{2,1,0:T(8,128)(2,1)}, u32[]{:S(2)}, u32[]{:S(2)}) async-start(bf16[16,64,2048]{2,1,0:T(8,128)(2,1)} %bitcast.150), calls=%async_computation.1 | async-start | bytes 8388608 | tf_op jit(solution)/shard_map/all_to_all | solution.py:162
  200.7 92.3 %copy-start.9 = (bf16[1,128,2048]{2,1,0:T(8,128)(2,1)S(1)}, bf16[1,128,2048]{2,1,0:T(8,128)(2,1)}, u32[]{:S(2)}) copy-start(bf16[1,128,2048]{2,1,0:T(8,128)(2,1)} %param.12) | copy-start | bytes 1572868
  200.7 92.3 %copy-start.12 = (f32[2048]{0:T(1024)S(1)}, f32[2048]{0:T(1024)}, u32[]{:S(2)}) copy-start(f32[2048]{0:T(1024)} %param.14) | copy-start | bytes 24580
  206.3 90.3 %copy-start.3 = (bf16[1,128,128]{2,1,0:T(8,128)(2,1)S(1)}, bf16[1,128,128]{2,1,0:T(8,128)(2,1)}, u32[]{:S(2)}) copy-start(bf16[1,128,128]{2,1,0:T(8,128)(2,1)} %param.22) | copy-start | bytes 98308
  293.0 3.2 copy-start.8
  293.0 3.2 copy-start.10
  296.2 1.2 copy-start.11
  297.4 9.5 %copy-start.1 = (bf16[128,2048]{1,0:T(8,128)(2,1)}, bf16[128,2048]{1,0:T(8,128)(2,1)S(1)}, u32[]{:S(2)}) copy-start(bf16[128,2048]{1,0:T(8,128)(2,1)S(1)} %add_convert_fusion.dy_ref) | copy-start | bytes 1572868
  297.4 6.9 %copy-start.4 = (bf16[1,128,128]{2,1,0:T(8,128)(2,1)S(1)}, bf16[1,128,128]{2,1,0:T(8,128)(2,1)}, u32[]{:S(2)}) copy-start(bf16[1,128,128]{2,1,0:T(8,128)(2,1)} %param.21) | copy-start | bytes 98308
  298.6 16.3 %collective-permute-start.11 = (bf16[128,2048]{0,1:T(8,128)(2,1)}, bf16[128,2048]{0,1:T(8,128)(2,1)}, u32[]{:S(2)}, u32[]{:S(2)}) collective-permute-start(bf16[128,2048]{0,1:T(8,128)(2,1)} %fusion.13), channel_id=1, source_target_pairs={{16,0},{17,1},{18,2},{19,3},{20,4},{21,5},{22,6},{23,7},{24,8},{25... | collective-permute-start | bytes 1572872 | tf_op jit(solution)/shard_map/ppermute | solution.py:62
  304.3 1.0 copy-start.2
  305.3 11.9 %copy-start.6 = (f32[128,2048]{1,0:T(8,128)S(1)}, f32[128,2048]{1,0:T(8,128)}, u32[]{:S(2)}) copy-start(f32[128,2048]{1,0:T(8,128)} %copy.73) | copy-start | bytes 3145732
Sparse Core Ops, SparseCore 0:
  10.9 127.1 all-gather.1

commit v5 on v4

--- a/solution.py
+++ b/solution.py
@@ -72,15 +72,13 @@
     return carried.astype(BF16)
 
 
-def gather_beside(rows):
+def gather_groups(rows):
     count = lax.axis_size("exp")
     if count != 16:
-        return lax.all_gather(rows, "exp")
-    depth = count // 4
-    me = lax.axis_index("exp")
-    z, x, core = me // 4, (me // 2) % 2, me % 2
-    out = jnp.zeros((depth, 2, 2) + rows.shape, rows.dtype)
-    for step in range(depth):
+        return [lax.all_gather(rows, "exp")]
+    x, core = (lax.axis_index("exp") // 2) % 2, lax.axis_index("exp") % 2
+    groups = []
+    for step in range(count // 4):
         block = rows
         if step:
             block = lax.ppermute(rows, "exp", [(i, (i + 4 * step) % count) for i in range(count)])
@@ -90,8 +88,20 @@
         quad = jnp.where(
             core == 0, jnp.stack([pair, swapped], 1), jnp.stack([swapped, pair], 1)
         )
-        out = lax.dynamic_update_index_in_dim(out, quad, (z - step + depth) % depth, 0)
-    return out.reshape((count,) + rows.shape)
+        groups.append(quad.reshape((4,) + rows.shape))
+    return groups
+
+
+def regroup(array, groups):
+    if groups == 1:
+        return array
+    own = lax.axis_index("exp") // (array.shape[0] // groups)
+    parted = array.reshape((groups, array.shape[0] // groups) + array.shape[1:])
+    picked = [
+        lax.dynamic_index_in_dim(parted, lax.rem(own - g + groups, groups), 0)
+        for g in range(groups)
+    ]
+    return jnp.concatenate(picked).reshape(array.shape)
 
 
 def local(
@@ -125,7 +135,7 @@
         jnp.where(routes[0][None] == names[:, None, None], gates[0][None], 0.0), axis=2
     )
     own_gates = lax.all_to_all(table, "exp", split_axis=0, concat_axis=0, tiled=True)
-    all_normed = lax.all_gather(normed, "exp")
+    all_normed = gather_groups(normed)
 
     before = jnp.triu(jnp.ones((tokens, tokens), BF16), 1)
     places = jnp.arange(capacity, dtype=jnp.int32)[None, :, None]
@@ -136,17 +146,27 @@
         return (slots[:, None, :] == places) & chosen[:, None, :]
 
     sent = picks(table).astype(BF16).reshape(experts * capacity, tokens)
-    all_grads = gather_beside(grads)
+    all_grads = gather_groups(grads)
+    groups = len(all_grads)
+    own_gates = regroup(own_gates, groups)
 
     held = picks(own_gates)
     slot_gates = jnp.sum(jnp.where(held, own_gates[:, None, :], 0.0), axis=2).reshape(-1, 1)
     onehot = held.astype(BF16)
 
-    def take(rows):
-        taken = lax.dot_general(
-            onehot, rows, (((2,), (1,)), ((0,), (0,))), preferred_element_type=F32
-        )
-        return taken.astype(BF16).reshape(experts * capacity, width)
+    each = experts // groups
+
+    def take(blocks):
+        taken = [
+            lax.dot_general(
+                onehot[g * each : (g + 1) * each],
+                rows,
+                (((2,), (1,)), ((0,), (0,))),
+                preferred_element_type=F32,
+            ).astype(BF16)
+            for g, rows in enumerate(blocks)
+        ]
+        return jnp.concatenate(taken).reshape(experts * capacity, width)
 
     normed_rows = take(all_normed)
     grad_rows = take(all_grads)
@@ -159,6 +179,7 @@
     grad_up = (back * gate_pre * sig).astype(BF16)
     summed = dot(grad_gate, gate_weight, 1, 1) + dot(grad_up, up_weight, 1, 1)
     weighted = (slot_gates * summed).astype(BF16).reshape(experts, capacity, width)
+    weighted = regroup(weighted, groups)
     returned = lax.all_to_all(weighted, "exp", split_axis=0, concat_axis=0, tiled=True)
     normed_grad = dot(sent, returned.reshape(experts * capacity, width), 0, 0)
 

time: 327 us -> 304 us (0.930)
  between operations: 14.3 us -> 1.13 us
  local copies, waits for them, and re-layouts: 26.2 us -> 16.3 us
  waiting for transfers between devices: 179 us -> 172 us
  starting transfers between devices: 26.6 us -> 33.5 us
  matrix products: 51.2 us -> 45.5 us
  other arithmetic: 27.8 us -> 33.1 us
    ppermute x11 -> x22, waiting for transfers between devices: 68.1 us -> 47.5 us  [the longest x6 32.1 us: gather_groups(): lax.ppermute(rows, 'exp', [(i, (i + 4 * step) % count) for i in range(cou...]
    all_to_all x1, waiting for transfers between devices: 15.8 us -> 29.1 us  [local(): lax.all_to_all(table, 'exp', split_axis=0, concat_axis=0, tiled=True)]
    select_n x4 -> x21, other arithmetic: 7.49 us -> 18.7 us  [the longest x13 16 us: gather_groups(): jnp.where(x == 0, jnp.stack([block, other]), jnp.stack([other, block]))]
    dynamic_update_slice x4 -> x0, other arithmetic: 9.12 us -> none  [gather_beside(): lax.dynamic_update_index_in_dim(out, quad, (z - step + depth) % depth, 0)]
    dynamic_update_slice x1 -> x0, local copies, waits for them, and re-layouts: 8.26 us -> none  [gather_beside(): lax.dynamic_update_index_in_dim(out, quad, (z - step + depth) % depth, 0)]
    dot_general x2 -> x8, matrix products: 9.54 us -> 3.51 us  [take(): lax.dot_general(onehot[g * each:(g + 1) * each], rows, (((2,), (1,)), ((0...]
    ppermute x11 -> x22, starting transfers between devices: 12.5 us -> 18.4 us  [the longest x6 8.64 us: gather_groups(): lax.ppermute(rows, 'exp', [(i, (i + 4 * step) % count) for i in range(cou...]
    concatenate x0 -> x4, other arithmetic: none -> 5.49 us  [the longest x2 3.17 us: take(): return jnp.concatenate(taken).reshape(experts * capacity, width)]
  transfers between devices with their start and end apart: 15 -> 25, of which waited for: 6 -> 8; matrix products, arithmetic and copies ran while one was open for 17% -> 14% of each run, Pallas kernels for 0% -> 1%
where the time goes in v5:
time: 304 us; the launch traced here: 303 us
  waiting for transfers between devices  172 us (57%)
  matrix products  45.5 us (15%)
  starting transfers between devices  33.5 us (11%)
  other arithmetic  33.1 us (11%)
  local copies, waits for them, and re-layouts  16.3 us (5%)
    all_to_all x1, waiting for transfers between devices, local(): lax.all_to_all(weighted, 'exp', split_axis=0, concat_axis=0, tiled=True)  86.8 us
    dot_general x10, matrix products, dot(): lax.dot_general(a, b, (((ca,), (cb,)), ((), ())), preferred_element_type=...  41.7 us
    ppermute x6, waiting for transfers between devices, gather_groups(): lax.ppermute(rows, 'exp', [(i, (i + 4 * step) % count) for i in range(cou...  32.1 us
    all_to_all x1, waiting for transfers between devices, local(): lax.all_to_all(table, 'exp', split_axis=0, concat_axis=0, tiled=True)  29.1 us
    select_n x13, other arithmetic, gather_groups(): jnp.where(x == 0, jnp.stack([block, other]), jnp.stack([other, block]))  16 us
    ppermute x8, waiting for transfers between devices, gather_groups(): other = lax.ppermute(block, 'exp', [(i, i ^ 2) for i in range(count)])  15.3 us
    ppermute x6, starting transfers between devices, gather_groups(): lax.ppermute(rows, 'exp', [(i, (i + 4 * step) % count) for i in range(cou...  8.64 us
    ppermute x8, starting transfers between devices, gather_groups(): other = lax.ppermute(block, 'exp', [(i, i ^ 2) for i in range(count)])  8.2 us
  transfers between devices with their start and end apart: 25, of which 8 were waited for; matrix products, arithmetic and copies ran while one was open for 14% of the time, Pallas kernels for 1%

profile of v5, /device:TPU:10, one launch (start us, length us, event | category | flops | bytes accessed | tf_op | source)
XLA Modules:
  0.0 302.7 jit_solution(9289979142741868597)
XLA Ops:
  0.7 1.6 collective-permute-start.2
  2.3 1.2 collective-permute-start.5
  3.5 1.8 collective-permute-start.8
  7.8 5.6 %all-to-all-start = ((f32[16,1,128]{2,1,0:T(1,128)}), f32[16,1,128]{2,1,0:T(1,128)S(1)}, u32[]{:S(2)}, u32[]{:S(2)}) async-start(f32[16,1,128]{2,1,0:T(1,128)} %bitcast.2), calls=%async_computation | async-start | bytes 16384 | tf_op jit(solution)/shard_map/all_to_all | solution.py:137
  13.4 1.2 fusion.21
  14.7 2.1 multiply_convert_fusion.6
  17.3 2.1 fusion.98
  20.3 29.1 %all-to-all-done = f32[16,1,128]{2,1,0:T(1,128)S(1)} async-done(((f32[16,1,128]{2,1,0:T(1,128)}), f32[16,1,128]{2,1,0:T(1,128)S(1)}, u32[]{:S(2)}, u32[]{:S(2)}) %all-to-all-start) | async-done | bytes 8224 | tf_op jit(solution)/shard_map/all_to_all | solution.py:137
  50.5 1.5 collective-permute-start.6
  52.0 1.8 maximum_select_fusion.9
  53.8 3.2 %collective-permute-start.16 = (bf16[128,2048]{1,0:T(8,128)(2,1)}, bf16[128,2048]{1,0:T(8,128)(2,1)S(1)}, u32[]{:S(2)}, u32[]{:S(2)}) collective-permute-start(bf16[128,2048]{1,0:T(8,128)(2,1)} %multiply_convert_fusion.6), channel_id=1, source_target_pairs={{0,8},{1,9},{2,10},{3,11},{4,12},{5,13},{6,14},{7,15},{8,0},{9,1},... | collective-permute-start | bytes 1572872 | tf_op jit(solution)/shard_map/ppermute | solution.py:84
  57.5 1.4 maximum_select_fusion.8
  59.1 5.6 %collective-permute-done.13 = bf16[128,2048]{1,0:T(8,128)(2,1)} collective-permute-done((bf16[128,2048]{1,0:T(8,128)(2,1)}, bf16[128,2048]{1,0:T(8,128)(2,1)}, u32[]{:S(2)}, u32[]{:S(2)}) %collective-permute-start.13) | collective-permute-done | bytes 524320 | tf_op jit(solution)/shard_map/ppermute | solution.py:84
  64.7 1.4 collective-permute-start.9
  66.1 1.4 maximum_select_fusion.15
  68.2 1.4 maximum_select_fusion.13
  69.5 25.8 %collective-permute-done.16 = bf16[128,2048]{1,0:T(8,128)(2,1)S(1)} collective-permute-done((bf16[128,2048]{1,0:T(8,128)(2,1)}, bf16[128,2048]{1,0:T(8,128)(2,1)S(1)}, u32[]{:S(2)}, u32[]{:S(2)}) %collective-permute-start.16) | collective-permute-done | bytes 524320 | tf_op jit(solution)/shard_map/ppermute | solution.py:84
  95.4 1.5 collective-permute-start.17
  96.8 1.4 maximum_select_fusion.11
  98.9 1.5 collective-permute-start.20
  100.4 1.4 maximum_select_fusion.14
  102.1 1.4 maximum_select_fusion.17
  103.4 6.7 %collective-permute-done.17 = bf16[128,2048]{1,0:T(8,128)(2,1)S(1)} collective-permute-done((bf16[128,2048]{1,0:T(8,128)(2,1)S(1)}, bf16[128,2048]{1,0:T(8,128)(2,1)S(1)}, u32[]{:S(2)}, u32[]{:S(2)}) %collective-permute-start.17) | collective-permute-done | bytes 524320 | tf_op jit(solution)/shard_map/ppermute | solution.py:85
  110.3 2.0 maximum_select_fusion.10
  112.3 8.7 %collective-permute-done.20 = bf16[128,2048]{1,0:T(8,128)(2,1)S(1)} collective-permute-done((bf16[128,2048]{1,0:T(8,128)(2,1)S(1)}, bf16[128,2048]{1,0:T(8,128)(2,1)S(1)}, u32[]{:S(2)}, u32[]{:S(2)}) %collective-permute-start.20) | collective-permute-done | bytes 524320 | tf_op jit(solution)/shard_map/ppermute | solution.py:85
  122.0 1.9 fusion.24
  123.9 1.6 maximum_select_fusion.16
  135.6 1.0 copy-done.14
  136.6 4.7 %fusion.7 = f32[1024,704]{0,1:T(8,128)} fusion(bf16[1024,2048]{1,0:T(8,128)(2,1)S(1)} %bitcast.193, bf16[1,704,2048]{2,1,0:T(8,128)(2,1)S(1)} %copy-done.14), kind=kOutput, calls=%fused_computation.11 | convolution fusion | flops 2952790016 | bytes 9961472 | tf_op jit(solution)/shard_map/dot_general | solution.py:17
  141.4 2.4 pad_maximum_fusion.1
  144.6 6.9 %fusion.2 = f32[1024,704]{0,1:T(8,128)} fusion(bf16[1024,2048]{1,0:T(8,128)(2,1)} %bitcast.60, bf16[1,2048,704]{1,2,0:T(8,128)(2,1)S(1)} %copy-done.15), kind=kOutput, calls=%fused_computation.6 | convolution fusion | flops 2952790016 | bytes 9961472 | tf_op jit(solution)/shard_map/dot_general | solution.py:17
  151.6 13.7 %fusion = f32[1024,2048]{1,0:T(8,128)} fusion(bf16[1,2048,704]{1,2,0:T(8,128)(2,1)} %param.17, f32[1024,704]{0,1:T(8,128)} %fusion.2, f32[1024,704]{0,1:T(8,128)} %fusion.7, bf16[1024,2048]{1,0:T(8,128)(2,1)} %bitcast.60, bf16[1,2048,704]{1,2,0:T(8,128)(2,1)S(1)} %copy-done), kind=kOutput, calls=%fused_computation.4 | convolution fusion | flops 5912788992 | bytes 24117248 | tf_op jit(solution)/shard_map/dot_general | solution.py:17
  165.2 7.7 %multiply_convert_fusion = bf16[1024,2048]{1,0:T(8,128)(2,1)S(1)} fusion(f32[1024,2048]{1,0:T(8,128)} %fusion, f32[1024]{0:T(1024)S(1)} %mul.70, bf16[1,2048,704]{1,2,0:T(8,128)(2,1)S(1)} %copy-done, f32[1024,704]{0,1:T(8,128)} %fusion.7, f32[1024,704]{0,1:T(8,128)} %fusion.2), kind=kOutput, calls=%fused_computation | convolution fusion | flops 2963406848 | bytes 21237760 | tf_op jit(solution)/shard_map/dot_general | solution.py:17
  173.5 2.3 pad_maximum_fusion.2
  175.8 8.1 %all-to-all-start.1 = ((bf16[16,64,2048]{2,1,0:T(8,128)(2,1)}), bf16[16,64,2048]{2,1,0:T(8,128)(2,1)}, u32[]{:S(2)}, u32[]{:S(2)}) async-start(bf16[16,64,2048]{2,1,0:T(8,128)(2,1)} %bitcast.178), calls=%async_computation.1 | async-start | bytes 8388608 | tf_op jit(solution)/shard_map/all_to_all | solution.py:183
  185.0 1.1 broadcast_in_dim.76
  186.1 2.6 copy.85
  189.5 86.8 %all-to-all-done.1 = bf16[16,64,2048]{2,1,0:T(8,128)(2,1)} async-done(((bf16[16,64,2048]{2,1,0:T(8,128)(2,1)}), bf16[16,64,2048]{2,1,0:T(8,128)(2,1)}, u32[]{:S(2)}, u32[]{:S(2)}) %all-to-all-start.1) | async-done | bytes 4194336 | tf_op jit(solution)/shard_map/all_to_all | solution.py:183
  276.3 3.2 %multiply_reduce_fusion = (f32[128]{0:T(128)S(1)}, f32[128,2048]{1,0:T(8,128)S(1)}) fusion(f32[128]{0:T(128)S(1)} %add_sqrt_fusion, bf16[1,128,2048]{2,1,0:T(8,128)(2,1)S(1)} %copy-done.5, f32[2048]{0:T(1024)S(1)} %copy-done.13, bf16[16,64,2048]{2,1,0:T(8,128)(2,1)} %all-to-all-done.1, s32[16,128]{1,0:T(8,128)S(1)} %convolution_convert_fusion.10, ...), kind=kOutput, calls=%fused_computation.78 | convolution fusion | flops 538443648 | bytes 5786624 | tf_op jit(solution)/shard_map/dot_general | solution.py:17
  280.8 1.2 fusion.13
  281.9 1.4 collective-permute-start.22
  283.5 1.8 broadcast_in_dim.75
  285.2 2.5 copy.87
  287.8 1.0 copy-done.2
  288.8 1.6 shard_map.139
  290.4 8.2 %collective-permute-done.22 = bf16[128,2048]{0,1:T(8,128)(2,1)} collective-permute-done((bf16[128,2048]{0,1:T(8,128)(2,1)}, bf16[128,2048]{0,1:T(8,128)(2,1)}, u32[]{:S(2)}, u32[]{:S(2)}) %collective-permute-start.22) | collective-permute-done | bytes 524320 | tf_op jit(solution)/shard_map/ppermute | solution.py:62
  298.6 2.0 fusion.20
  300.5 2.1 fusion.14
  (112 shorter events, 23.4 us)
Async XLA Ops:
  0.6 150.9 %copy-start = (bf16[1,2048,704]{1,2,0:T(8,128)(2,1)S(1)}, bf16[1,2048,704]{1,2,0:T(8,128)(2,1)}, u32[]{:S(2)}) copy-start(bf16[1,2048,704]{1,2,0:T(8,128)(2,1)} %param.18) | copy-start | bytes 8650756
  0.6 18.7 %copy-start.5 = (bf16[1,128,2048]{2,1,0:T(8,128)(2,1)S(1)}, bf16[1,128,2048]{2,1,0:T(8,128)(2,1)}, u32[]{:S(2)}) copy-start(bf16[1,128,2048]{2,1,0:T(8,128)(2,1)} %param.12) | copy-start | bytes 1572868
  0.7 18.7 %copy-start.13 = (f32[2048]{0:T(1024)S(1)}, f32[2048]{0:T(1024)}, u32[]{:S(2)}) copy-start(f32[2048]{0:T(1024)} %param.14) | copy-start | bytes 24580
  0.7 53.1 %collective-permute-start.2 = (bf16[128,2048]{1,0:T(8,128)(2,1)}, bf16[128,2048]{1,0:T(8,128)(2,1)}, u32[]{:S(2)}, u32[]{:S(2)}) collective-permute-start(bf16[128,2048]{1,0:T(8,128)(2,1)} %bitcast.187), channel_id=1, source_target_pairs={{0,4},{1,5},{2,6},{3,7},{4,8},{5,9},{6,10},{7,11},{8,12},{9,13},{1... | collective-permute-start | bytes 1572872 | tf_op jit(solution)/shard_map/ppermute | solution.py:84
  2.3 47.3 %collective-permute-start.5 = (bf16[128,2048]{1,0:T(8,128)(2,1)}, bf16[128,2048]{1,0:T(8,128)(2,1)}, u32[]{:S(2)}, u32[]{:S(2)}) collective-permute-start(bf16[128,2048]{1,0:T(8,128)(2,1)} %bitcast.188), channel_id=1, source_target_pairs={{0,8},{1,9},{2,10},{3,11},{4,12},{5,13},{6,14},{7,15},{8,0},{9,1},... | collective-permute-start | bytes 1572872 | tf_op jit(solution)/shard_map/ppermute | solution.py:84
  3.5 55.3 %collective-permute-start.8 = (bf16[128,2048]{1,0:T(8,128)(2,1)}, bf16[128,2048]{1,0:T(8,128)(2,1)}, u32[]{:S(2)}, u32[]{:S(2)}) collective-permute-start(bf16[128,2048]{1,0:T(8,128)(2,1)} %bitcast.189), channel_id=1, source_target_pairs={{0,12},{1,13},{2,14},{3,15},{4,0},{5,1},{6,2},{7,3},{8,4},{9,5},{1... | collective-permute-start | bytes 1572872 | tf_op jit(solution)/shard_map/ppermute | solution.py:84
  5.3 45.1 %collective-permute-start = (bf16[128,2048]{1,0:T(8,128)(2,1)}, bf16[128,2048]{1,0:T(8,128)(2,1)}, u32[]{:S(2)}, u32[]{:S(2)}) collective-permute-start(bf16[128,2048]{1,0:T(8,128)(2,1)} %bitcast.190), channel_id=1, source_target_pairs={{0,2},{1,3},{2,0},{3,1},{4,6},{5,7},{6,4},{7,5},{8,10},{9,11},{10,... | collective-permute-start | bytes 1572872 | tf_op jit(solution)/shard_map/ppermute | solution.py:85
  7.8 41.6 %all-to-all-start = ((f32[16,1,128]{2,1,0:T(1,128)}), f32[16,1,128]{2,1,0:T(1,128)S(1)}, u32[]{:S(2)}, u32[]{:S(2)}) async-start(f32[16,1,128]{2,1,0:T(1,128)} %bitcast.2), calls=%async_computation | async-start | bytes 16384 | tf_op jit(solution)/shard_map/all_to_all | solution.py:137
  16.7 40.2 %collective-permute-start.11 = (bf16[128,2048]{1,0:T(8,128)(2,1)}, bf16[128,2048]{1,0:T(8,128)(2,1)}, u32[]{:S(2)}, u32[]{:S(2)}) collective-permute-start(bf16[128,2048]{1,0:T(8,128)(2,1)} %multiply_convert_fusion.6), channel_id=1, source_target_pairs={{0,2},{1,3},{2,0},{3,1},{4,6},{5,7},{6,4},{7,5},{8,10},{9,11},{10,... | collective-permute-start | bytes 1572872 | tf_op jit(solution)/shard_map/ppermute | solution.py:85
  49.6 15.1 %collective-permute-start.13 = (bf16[128,2048]{1,0:T(8,128)(2,1)}, bf16[128,2048]{1,0:T(8,128)(2,1)}, u32[]{:S(2)}, u32[]{:S(2)}) collective-permute-start(bf16[128,2048]{1,0:T(8,128)(2,1)} %multiply_convert_fusion.6), channel_id=1, source_target_pairs={{0,4},{1,5},{2,6},{3,7},{4,8},{5,9},{6,10},{7,11},{8,12},{9,13},{1... | collective-permute-start | bytes 1572872 | tf_op jit(solution)/shard_map/ppermute | solution.py:84
  50.5 7.0 %copy-start.8 = (bf16[1,128,2048]{2,1,0:T(8,128)(2,1)S(1)}, bf16[1,128,2048]{2,1,0:T(8,128)(2,1)}, u32[]{:S(2)}) copy-start(bf16[1,128,2048]{2,1,0:T(8,128)(2,1)} %param.13) | copy-start | bytes 1572868
  50.5 17.0 %collective-permute-start.6 = (bf16[128,2048]{1,0:T(8,128)(2,1)}, bf16[128,2048]{1,0:T(8,128)(2,1)S(1)}, u32[]{:S(2)}, u32[]{:S(2)}) collective-permute-start(bf16[128,2048]{1,0:T(8,128)(2,1)} %collective-permute-done.5), channel_id=1, source_target_pairs={{0,2},{1,3},{2,0},{3,1},{4,6},{5,7},{6,4},{7,5},{8,10},{9,11},{10,... | collective-permute-start | bytes 1572872 | tf_op jit(solution)/shard_map/ppermute | solution.py:85
  52.0 14.1 %copy-start.12 = (bf16[1,128,2048]{2,1,0:T(8,128)(2,1)S(1)}, bf16[1,128,2048]{2,1,0:T(8,128)(2,1)}, u32[]{:S(2)}) copy-start(bf16[1,128,2048]{2,1,0:T(8,128)(2,1)} %fusion.23) | copy-start | bytes 1572868
  53.8 41.6 %collective-permute-start.16 = (bf16[128,2048]{1,0:T(8,128)(2,1)}, bf16[128,2048]{1,0:T(8,128)(2,1)S(1)}, u32[]{:S(2)}, u32[]{:S(2)}) collective-permute-start(bf16[128,2048]{1,0:T(8,128)(2,1)} %multiply_convert_fusion.6), channel_id=1, source_target_pairs={{0,8},{1,9},{2,10},{3,11},{4,12},{5,13},{6,14},{7,15},{8,0},{9,1},... | collective-permute-start | bytes 1572872 | tf_op jit(solution)/shard_map/ppermute | solution.py:84
  56.9 38.4 %collective-permute-start.3 = (bf16[128,2048]{1,0:T(8,128)(2,1)}, bf16[128,2048]{1,0:T(8,128)(2,1)S(1)}, u32[]{:S(2)}, u32[]{:S(2)}) collective-permute-start(bf16[128,2048]{1,0:T(8,128)(2,1)} %collective-permute-done.2), channel_id=1, source_target_pairs={{0,2},{1,3},{2,0},{3,1},{4,6},{5,7},{6,4},{7,5},{8,10},{9,11},{10,... | collective-permute-start | bytes 1572872 | tf_op jit(solution)/shard_map/ppermute | solution.py:85
  58.9 40.0 %collective-permute-start.19 = (bf16[128,2048]{1,0:T(8,128)(2,1)}, bf16[128,2048]{1,0:T(8,128)(2,1)S(1)}, u32[]{:S(2)}, u32[]{:S(2)}) collective-permute-start(bf16[128,2048]{1,0:T(8,128)(2,1)} %multiply_convert_fusion.6), channel_id=1, source_target_pairs={{0,12},{1,13},{2,14},{3,15},{4,0},{5,1},{6,2},{7,3},{8,4},{9,5},{1... | collective-permute-start | bytes 1572872 | tf_op jit(solution)/shard_map/ppermute | solution.py:84
  64.7 34.2 %collective-permute-start.9 = (bf16[128,2048]{1,0:T(8,128)(2,1)}, bf16[128,2048]{1,0:T(8,128)(2,1)S(1)}, u32[]{:S(2)}, u32[]{:S(2)}) collective-permute-start(bf16[128,2048]{1,0:T(8,128)(2,1)} %collective-permute-done.8), channel_id=1, source_target_pairs={{0,2},{1,3},{2,0},{3,1},{4,6},{5,7},{6,4},{7,5},{8,10},{9,11},{10,... | collective-permute-start | bytes 1572872 | tf_op jit(solution)/shard_map/ppermute | solution.py:85
  67.5 34.3 %collective-permute-start.14 = (bf16[128,2048]{1,0:T(8,128)(2,1)}, bf16[128,2048]{1,0:T(8,128)(2,1)S(1)}, u32[]{:S(2)}, u32[]{:S(2)}) collective-permute-start(bf16[128,2048]{1,0:T(8,128)(2,1)} %collective-permute-done.13), channel_id=1, source_target_pairs={{0,2},{1,3},{2,0},{3,1},{4,6},{5,7},{6,4},{7,5},{8,10},{9,11},{10,... | collective-permute-start | bytes 1572872 | tf_op jit(solution)/shard_map/ppermute | solution.py:85
  95.4 30.1 %collective-permute-start.1 = (bf16[2,128,2048]{2,1,0:T(8,128)(2,1)S(1)}, bf16[2,128,2048]{2,1,0:T(8,128)(2,1)S(1)}, u32[]{:S(2)}, u32[]{:S(2)}) collective-permute-start(bf16[2,128,2048]{2,1,0:T(8,128)(2,1)S(1)} %maximum_select_fusion.9), channel_id=1, source_target_pairs={{0,1},{1,0},{2,3},{3,2},{4,5},{5,4},{6,7},{7,6},{8,9},{9,8},{10,11... | collective-permute-start | bytes 3145736 | tf_op jit(solution)/shard_map/ppermute | solution.py:87
  95.4 14.7 %collective-permute-start.17 = (bf16[128,2048]{1,0:T(8,128)(2,1)S(1)}, bf16[128,2048]{1,0:T(8,128)(2,1)S(1)}, u32[]{:S(2)}, u32[]{:S(2)}) collective-permute-start(bf16[128,2048]{1,0:T(8,128)(2,1)S(1)} %collective-permute-done.16), channel_id=1, source_target_pairs={{0,2},{1,3},{2,0},{3,1},{4,6},{5,7},{6,4},{7,5},{8,10},{9,11},{10,... | collective-permute-start | bytes 1572872 | tf_op jit(solution)/shard_map/ppermute | solution.py:85
  98.9 27.8 %collective-permute-start.12 = (bf16[2,128,2048]{2,1,0:T(8,128)(2,1)S(1)}, bf16[2,128,2048]{2,1,0:T(8,128)(2,1)S(1)}, u32[]{:S(2)}, u32[]{:S(2)}) collective-permute-start(bf16[2,128,2048]{2,1,0:T(8,128)(2,1)S(1)} %maximum_select_fusion.15), channel_id=1, source_target_pairs={{0,1},{1,0},{2,3},{3,2},{4,5},{5,4},{6,7},{7,6},{8,9},{9,8},{10,11... | collective-permute-start | bytes 3145736 | tf_op jit(solution)/shard_map/ppermute | solution.py:87
  98.9 22.0 %collective-permute-start.20 = (bf16[128,2048]{1,0:T(8,128)(2,1)S(1)}, bf16[128,2048]{1,0:T(8,128)(2,1)S(1)}, u32[]{:S(2)}, u32[]{:S(2)}) collective-permute-start(bf16[128,2048]{1,0:T(8,128)(2,1)S(1)} %collective-permute-done.19), channel_id=1, source_target_pairs={{0,2},{1,3},{2,0},{3,1},{4,6},{5,7},{6,4},{7,5},{8,10},{9,11},{10,... | collective-permute-start | bytes 1572872 | tf_op jit(solution)/shard_map/ppermute | solution.py:85
  101.8 26.3 %collective-permute-start.7 = (bf16[2,128,2048]{2,1,0:T(8,128)(2,1)S(1)}, bf16[2,128,2048]{2,1,0:T(8,128)(2,1)S(1)}, u32[]{:S(2)}, u32[]{:S(2)}) collective-permute-start(bf16[2,128,2048]{2,1,0:T(8,128)(2,1)S(1)} %maximum_select_fusion.13), channel_id=1, source_target_pairs={{0,1},{1,0},{2,3},{3,2},{4,5},{5,4},{6,7},{7,6},{8,9},{9,8},{10,11... | collective-permute-start | bytes 3145736 | tf_op jit(solution)/shard_map/ppermute | solution.py:87
  110.1 19.2 %collective-permute-start.4 = (bf16[2,128,2048]{2,1,0:T(8,128)(2,1)S(1)}, bf16[2,128,2048]{2,1,0:T(8,128)(2,1)S(1)}, u32[]{:S(2)}, u32[]{:S(2)}) collective-permute-start(bf16[2,128,2048]{2,1,0:T(8,128)(2,1)S(1)} %maximum_select_fusion.11), channel_id=1, source_target_pairs={{0,1},{1,0},{2,3},{3,2},{4,5},{5,4},{6,7},{7,6},{8,9},{9,8},{10,11... | collective-permute-start | bytes 3145736 | tf_op jit(solution)/shard_map/ppermute | solution.py:87
  121.0 8.9 %collective-permute-start.10 = (bf16[2,128,2048]{2,1,0:T(8,128)(2,1)S(1)}, bf16[2,128,2048]{2,1,0:T(8,128)(2,1)S(1)}, u32[]{:S(2)}, u32[]{:S(2)}) collective-permute-start(bf16[2,128,2048]{2,1,0:T(8,128)(2,1)S(1)} %maximum_select_fusion.14), channel_id=1, source_target_pairs={{0,1},{1,0},{2,3},{3,2},{4,5},{5,4},{6,7},{7,6},{8,9},{9,8},{10,11... | collective-permute-start | bytes 3145736 | tf_op jit(solution)/shard_map/ppermute | solution.py:87
  121.0 1.0 copy-start.11
  125.5 4.8 %collective-permute-start.15 = (bf16[2,128,2048]{2,1,0:T(8,128)(2,1)S(1)}, bf16[2,128,2048]{2,1,0:T(8,128)(2,1)S(1)}, u32[]{:S(2)}, u32[]{:S(2)}) collective-permute-start(bf16[2,128,2048]{2,1,0:T(8,128)(2,1)S(1)} %maximum_select_fusion.17), channel_id=1, source_target_pairs={{0,1},{1,0},{2,3},{3,2},{4,5},{5,4},{6,7},{7,6},{8,9},{9,8},{10,11... | collective-permute-start | bytes 3145736 | tf_op jit(solution)/shard_map/ppermute | solution.py:87
  126.7 4.8 %collective-permute-start.18 = (bf16[2,128,2048]{2,1,0:T(8,128)(2,1)S(1)}, bf16[2,128,2048]{2,1,0:T(8,128)(2,1)S(1)}, u32[]{:S(2)}, u32[]{:S(2)}) collective-permute-start(bf16[2,128,2048]{2,1,0:T(8,128)(2,1)S(1)} %maximum_select_fusion.18), channel_id=1, source_target_pairs={{0,1},{1,0},{2,3},{3,2},{4,5},{5,4},{6,7},{7,6},{8,9},{9,8},{10,11... | collective-permute-start | bytes 3145736 | tf_op jit(solution)/shard_map/ppermute | solution.py:87
  128.1 5.8 %collective-permute-start.21 = (bf16[2,128,2048]{2,1,0:T(8,128)(2,1)S(1)}, bf16[2,128,2048]{2,1,0:T(8,128)(2,1)S(1)}, u32[]{:S(2)}, u32[]{:S(2)}) collective-permute-start(bf16[2,128,2048]{2,1,0:T(8,128)(2,1)S(1)} %maximum_select_fusion.20), channel_id=1, source_target_pairs={{0,1},{1,0},{2,3},{3,2},{4,5},{5,4},{6,7},{7,6},{8,9},{9,8},{10,11... | collective-permute-start | bytes 3145736 | tf_op jit(solution)/shard_map/ppermute | solution.py:87
  134.8 1.8 copy-start.14
  141.4 3.3 %copy-start.15 = (bf16[1,2048,704]{1,2,0:T(8,128)(2,1)S(1)}, bf16[1,2048,704]{1,2,0:T(8,128)(2,1)}, u32[]{:S(2)}) copy-start(bf16[1,2048,704]{1,2,0:T(8,128)(2,1)} %param.17) | copy-start | bytes 8650756
  175.8 8.1 %copy-start.16 = (f32[1,128,32]{1,2,0:T(8,128)S(1)}, f32[1,128,32]{1,2,0:T(8,128)}, u32[]{:S(2)}) copy-start(f32[1,128,32]{1,2,0:T(8,128)} %param.23) | copy-start | bytes 49156
  175.8 100.5 %all-to-all-start.1 = ((bf16[16,64,2048]{2,1,0:T(8,128)(2,1)}), bf16[16,64,2048]{2,1,0:T(8,128)(2,1)}, u32[]{:S(2)}, u32[]{:S(2)}) async-start(bf16[16,64,2048]{2,1,0:T(8,128)(2,1)} %bitcast.178), calls=%async_computation.1 | async-start | bytes 8388608 | tf_op jit(solution)/shard_map/all_to_all | solution.py:183
  276.3 3.2 %copy-start.6 = (bf16[1,128,2048]{2,1,0:T(8,128)(2,1)S(1)}, bf16[1,128,2048]{2,1,0:T(8,128)(2,1)}, u32[]{:S(2)}) copy-start(bf16[1,128,2048]{2,1,0:T(8,128)(2,1)} %param.12) | copy-start | bytes 1572868
  276.3 3.2 %copy-start.9 = (bf16[1,128,2048]{2,1,0:T(8,128)(2,1)S(1)}, bf16[1,128,2048]{2,1,0:T(8,128)(2,1)}, u32[]{:S(2)}) copy-start(bf16[1,128,2048]{2,1,0:T(8,128)(2,1)} %param.13) | copy-start | bytes 1572868
  279.5 0.8 copy-start.3
  279.5 1.2 copy-start.10
  280.8 7.0 %copy-start.1 = (bf16[128,2048]{1,0:T(8,128)(2,1)}, bf16[128,2048]{1,0:T(8,128)(2,1)S(1)}, u32[]{:S(2)}) copy-start(bf16[128,2048]{1,0:T(8,128)(2,1)S(1)} %add_convert_fusion.dy_ref) | copy-start | bytes 1572868
  281.9 5.8 %copy-start.4 = (bf16[1,128,128]{2,1,0:T(8,128)(2,1)S(1)}, bf16[1,128,128]{2,1,0:T(8,128)(2,1)}, u32[]{:S(2)}) copy-start(bf16[1,128,128]{2,1,0:T(8,128)(2,1)} %param.21) | copy-start | bytes 98308
  281.9 16.6 %collective-permute-start.22 = (bf16[128,2048]{0,1:T(8,128)(2,1)}, bf16[128,2048]{0,1:T(8,128)(2,1)}, u32[]{:S(2)}, u32[]{:S(2)}) collective-permute-start(bf16[128,2048]{0,1:T(8,128)(2,1)} %fusion.13), channel_id=1, source_target_pairs={{16,0},{17,1},{18,2},{19,3},{20,4},{21,5},{22,6},{23,7},{24,8},{25... | collective-permute-start | bytes 1572872 | tf_op jit(solution)/shard_map/ppermute | solution.py:62
  287.8 1.0 copy-start.2
  288.8 9.8 %copy-start.7 = (f32[128,2048]{1,0:T(8,128)S(1)}, f32[128,2048]{1,0:T(8,128)}, u32[]{:S(2)}) copy-start(f32[128,2048]{1,0:T(8,128)} %copy.87) | copy-start | bytes 3145732
